TPU v7x, 256 devices: a whole 4x4x8 slice. The times are simulated.
256 devices in a mesh: section: 4 (over x), tp: 16 (over z, core), dp: 4 (over y).
Axes of the slice: x: 4, y: 4, z: 8, core: 2. Of those that a mesh axis runs over, the one named last changes fastest.
Arguments:
- hidden_states: bfloat16 [672, 8192], P(None, 'dp'), may hold values from -120 to 120
- norm_gain: float32 [8192], P('dp'), may hold values from 0.5 to 1.5
- lm_head: bfloat16 [8192, 152064], P('dp', ('section', 'tp')), may hold values from -6 to 6
- target_ids: int32 [672], replicated, may hold values from 0 to 152063
Outputs:
- logprobs: bfloat16 [672, 152064], P(None, ('section', 'tp', 'dp'))
- target_logprob: float32 [672], P('dp')
All inputs are finite; a program needn't handle non-finite values.
Results may differ from a plain program's by a relative error of at most 0.0031.
Values may be sent and summed in bfloat16 or wider, within the bound.
No kernel may reach another device: no remote copies, remote signals or barrier semaphores. Data moves between devices by JAX's collectives and lax.ppermute only.
A program may use at most 128 MiB of HBM per device.

v0:
```python
import jax
import jax.numpy as jnp
from jax import lax
from jax.sharding import PartitionSpec as P

D = 8192


epsilon = 1e-06


def local_terms(logits, targets, offset):
    columns = lax.broadcasted_iota(jnp.int32, logits.shape, 1) + offset
    return jnp.sum(jnp.where(columns == targets[:, None], logits, 0.0), axis=1)


def body(hidden_states, norm_gain, lm_head, target_ids):
    widened = hidden_states.astype(jnp.float32)
    squares = lax.psum(jnp.sum(widened * widened, axis=1), "dp")
    scale = lax.rsqrt(squares / D + epsilon)
    normed = (widened * scale[:, None] * norm_gain[None, :]).astype(jnp.bfloat16)
    row_count = normed.shape[0]
    block_width = lm_head.shape[1]
    dp_size = lax.axis_size("dp")
    own_rows = row_count // dp_size
    group_index = lax.axis_index("section") * lax.axis_size("tp") + lax.axis_index("tp")
    logits = lax.psum_scatter(
        jnp.dot(normed, lm_head, preferred_element_type=jnp.float32),
        "dp",
        scatter_dimension=0,
        tiled=True,
    )
    targets = lax.dynamic_slice_in_dim(target_ids, lax.axis_index("dp") * own_rows, own_rows, 0)
    picked = local_terms(logits, targets, group_index * block_width)
    row_top = lax.pmax(jnp.max(logits, axis=1), ("section", "tp"))
    row_total, picked = lax.psum(
        (jnp.sum(jnp.exp(logits - row_top[:, None]), axis=1), picked), ("section", "tp")
    )
    shifted = (logits - row_top[:, None] - jnp.log(row_total)[:, None]).astype(jnp.bfloat16)
    logprobs = lax.all_to_all(shifted, "dp", split_axis=1, concat_axis=0, tiled=True)
    target_logprob = picked - row_top - jnp.log(row_total)
    return (logprobs, target_logprob)


def solution(mesh):
    placed = (P(None, "dp"), P("dp"), P("dp", ("section", "tp")), P())
    return jax.shard_map(
        body,
        mesh=mesh,
        in_specs=placed,
        out_specs=(P(None, ("section", "tp", "dp")), P("dp")),
        check_vma=False,
    )
```

profile of v0, /device:TPU:1, one launch (start us, length us, event | category | flops | bytes accessed | tf_op | source)
XLA Modules:
  0.0 383.7 jit_solution(5082792151609679468)
XLA Ops:
  7.2 0.0 copy-start.1
  7.2 0.0 copy-start.2
  7.2 0.0 reduce-scatter.4.cloned.1.call-start
  7.2 2.5 fusion
  9.8 9.6 %psum.21 = f32[672]{0:T(1024)S(1)} all-reduce(f32[672]{0:T(1024)S(1)} %fusion), channel_id=1, replica_groups=mesh['section'=4,'tp'=16,'dp'=4] {'dp'}, use_global_device_ids=true, to_apply=%region_1.0 | all-reduce | flops 672 | bytes 5376 | tf_op jit(solution)/shard_map/psum | solution.py:19
  19.3 0.0 copy-done.1
  19.3 0.0 copy-done.2
  19.3 11.7 %fusion.3 = f32[672,2376]{1,0:T(8,128)} fusion(bf16[2048,2376]{0,1:T(8,128)(2,1)} %param.6, bf16[672,2048]{1,0:T(8,128)(2,1)S(1)} %copy-done.1, f32[2048]{0:T(1024)S(1)} %copy-done.2, f32[672]{0:T(1024)S(1)} %add_rsqrt_fusion), kind=kOutput, calls=%fused_computation.5 | convolution fusion | flops 6545473536 | bytes 18882176 | tf_op jit(solution)/shard_map/dot_general | solution.py:28
  31.1 0.0 reduce-scatter.4.cloned.1.call-update
  31.1 0.8 dynamic_slice.3
  31.9 70.7 %reduce-scatter.4.cloned.1.call-done = f32[168,2376]{1,0:T(8,128)} async-done(((f32[672,2376]{1,0:T(8,128)}), f32[168,2376]{1,0:T(8,128)}) %reduce-scatter.4.cloned.1.call-update) | async-done | bytes 1596688
  102.6 0.0 copy-start
  102.6 1.7 reduce_max.9
  104.3 124.5 %pmax.7 = f32[168]{0:T(256)S(1)} all-reduce(f32[168]{0:T(256)S(1)} %reduce_max.9), channel_id=1, replica_groups=mesh['section'=4,'tp'=16,'dp'=4] {'section','tp'}, use_global_device_ids=true, to_apply=%region_4.5 | all-reduce | flops 168 | bytes 1344 | tf_op jit(solution)/shard_map/pmax | solution.py:35
  228.8 2.0 select_reduce_fusion
  230.8 128.5 %all-reduce.1 = (f32[168]{0:T(256)S(1)}, f32[168]{0:T(256)S(1)}) all-reduce(f32[168]{0:T(256)S(1)} %get-tuple-element.3, f32[168]{0:T(256)S(1)} %get-tuple-element.2), channel_id=1, replica_groups=mesh['section'=4,'tp'=16,'dp'=4] {'section','tp'}, use_global_device_ids=true, to_apply=%region_6.7 | all-reduce | flops 336 | bytes 2688 | tf_op jit(solution)/shard_map/psum | solution.py:36
  359.3 0.6 subtract_subtract_fusion
  359.9 0.0 copy-done
  359.9 0.3 subtract_convert_fusion
  360.1 0.9 all_to_all.14
  361.1 0.1 copy.7
  361.2 14.8 %all_to_all.19 = bf16[168,4,594]{2,0,1:T(8,128)(2,1)S(1)} all-to-all(bf16[168,4,594]{2,0,1:T(8,128)(2,1)S(1)} %copy.7), channel_id=1, replica_groups=mesh['section'=4,'tp'=16,'dp'=4] {'dp'}, dimensions={1} | all-to-all | bytes 1596672 | tf_op jit(solution)/shard_map/all_to_all | solution.py:40
  375.9 0.9 copy.9
  (2 shorter events, 0.0 us)
Async XLA Ops:
  7.2 12.2 %copy-start.1 = (bf16[672,2048]{1,0:T(8,128)(2,1)S(1)}, bf16[672,2048]{1,0:T(8,128)(2,1)}, u32[]{:S(2)}) copy-start(bf16[672,2048]{1,0:T(8,128)(2,1)} %param.4) | copy-start | bytes 8257540
  7.2 12.2 %copy-start.2 = (f32[2048]{0:T(1024)S(1)}, f32[2048]{0:T(1024)}, u32[]{:S(2)}) copy-start(f32[2048]{0:T(1024)} %param.5) | copy-start | bytes 24580
  7.2 95.4 %reduce-scatter.4.cloned.1.call-start = ((), (), s32[]{:S(2)}) async-start(), calls=%async_computation.2 | async-start | bytes 8171520
  102.6 257.3 %copy-start = (f32[168,2376]{1,0:T(8,128)S(1)}, f32[168,2376]{1,0:T(8,128)}, u32[]{:S(2)}) copy-start(f32[168,2376]{1,0:T(8,128)} %reduce-scatter.4.cloned.1.call-done) | copy-start | bytes 4790020
Sparse Core Ops, SparseCore 0:
  31.2 71.3 reduce-scatter.3
where the time goes:
time: 384 us
  blocking collectives  277 us (72%)
  waiting for transfers between devices  70.7 us (18%)
  between operations  14.1 us (4%)
  matrix products  11.7 us (3%)
  other arithmetic  7.08 us (2%)
    psum x1, blocking collectives, body(): lax.psum((jnp.sum(jnp.exp(logits - row_top[:, None]), axis=1), picked), (...  128 us
    pmax x1, blocking collectives, body(): row_top = lax.pmax(jnp.max(logits, axis=1), ('section', 'tp'))  125 us
    unnamed x2, waiting for transfers between devices  70.7 us
    all_to_all x1, blocking collectives, body(): lax.all_to_all(shifted, 'dp', split_axis=1, concat_axis=0, tiled=True)  14.8 us
    dot_general x1, matrix products, body(): jnp.dot(normed, lm_head, preferred_element_type=jnp.float32)  11.7 us
    psum x1, blocking collectives, body(): squares = lax.psum(jnp.sum(widened * widened, axis=1), 'dp')  9.56 us
  transfers between devices with their start and end apart: 1, of which 1 were waited for; matrix products, arithmetic and copies ran while one was open for 0% of the time, Pallas kernels for 0%

commit v1 on v0

v1 whole, which is shorter than its diff:
```python
import functools

import jax
import jax.numpy as jnp
from jax import lax
from jax.experimental import pallas as pl
from jax.experimental.pallas import tpu as pltpu
from jax.sharding import PartitionSpec as P

D = 8192
EPSILON = 1e-06
ROWS = 672
HALF = ROWS // 2
DP = 4
OWN = 594
STEP = 592
TAIL = 16
WIDE = 640
SQUARES = STEP + 8 - 512
VMEM = pltpu.CompilerParams(vmem_limit_bytes=50 * 1024 * 1024)
F32 = jnp.float32
BF16 = jnp.bfloat16


def whole():
    return pl.BlockSpec(memory_space=pltpu.VMEM)


def lane_of(shape):
    return lax.broadcasted_iota(jnp.int32, shape, 1)


def with_squares(tile, total):
    lane = lane_of(tile.shape)
    high = total.astype(BF16).astype(F32)
    middle = (total - high).astype(BF16).astype(F32)
    low = total - high - middle
    terms = jnp.where(lane == SQUARES, high, jnp.where(lane == SQUARES + 1, middle, low))
    return jnp.where(lane < SQUARES, tile, jnp.where(lane < SQUARES + 3, terms, 0.0))


def squares_of(tile):
    lane = lane_of(tile.shape)
    held = (lane >= SQUARES) & (lane < SQUARES + 3)
    return jnp.sum(jnp.where(held, tile, 0.0), axis=1, keepdims=True)


def window_dots(left, w_ref, t_ref, store):
    contract = (((1,), (1,)), ((), ()))
    for begin in (0, 256):
        store(begin, lax.dot_general(left, w_ref[begin : begin + 256, :], contract, preferred_element_type=F32))
    last = jnp.concatenate([w_ref[512:STEP, :], t_ref[...], w_ref[0:32, :]], axis=0)
    store(512, lax.dot_general(left, last, contract, preferred_element_type=F32))


def first_kernel(d_ref, x_ref, g_ref, w_ref, t_ref, hg_ref, sq_ref, up_ref, down_ref):
    half = pl.program_id(0)

    def prepare(i, _):
        rows = pl.ds(pl.multiple_of(i * 16, 16), 16)
        x = x_ref[rows, :].astype(F32)
        hg_ref[rows, :] = (x * g_ref[...]).astype(BF16)
        sq_ref[rows, :] = jnp.broadcast_to(jnp.sum(x * x, axis=1, keepdims=True), (16, 128))
        return 0

    lax.fori_loop(0, HALF // 16, prepare, 0)

    def compute(out_ref):
        def store(begin, product):
            if begin == 512:
                product = with_squares(product, sq_ref[:, 0:1])
            out_ref[:, begin : begin + product.shape[1]] = product.astype(BF16)

        window_dots(hg_ref[...], w_ref, t_ref, store)

    pl.when(half == 0)(lambda: compute(up_ref))
    pl.when(half == 1)(lambda: compute(down_ref))


def rest_kernel(d_ref, hg_ref, sq_ref, w_ref, t_ref, up_ref, up_held_ref, down_ref, down_held_ref, own_ref, res_ref):
    j = pl.program_id(0)
    for half in (0, 1):
        rows = slice(half * HALF, half * HALF + HALF)

        def store(begin, product):
            if begin == 512:
                product = with_squares(product, sq_ref[rows, 0:1])
            res_ref[rows, begin : begin + product.shape[1]] = product

        window_dots(hg_ref[rows, :], w_ref, t_ref, store)

    @pl.when(j == 0)
    def _():
        up_held_ref[...] = res_ref[:HALF, :]
        up_ref[...] = res_ref[HALF:, :].astype(BF16)

    @pl.when(j == 1)
    def _():
        down_ref[...] = res_ref[:HALF, :].astype(BF16)
        down_held_ref[...] = res_ref[HALF:, :]

    @pl.when(j == 2)
    def _():
        own_ref[...] = res_ref[...]


def add_kernel(up_in_ref, up_held_ref, down_in_ref, down_held_ref, up_ref, down_ref):
    for in_ref, held_ref, out_ref in ((up_in_ref, up_held_ref, up_ref), (down_in_ref, down_held_ref, down_ref)):

        def add(i, _):
            rows = pl.ds(pl.multiple_of(i * 16, 16), 16)
            out_ref[rows, :512] = (held_ref[rows, :512] + in_ref[rows, :512].astype(F32)).astype(BF16)
            came = in_ref[rows, 512:].astype(F32)
            held = held_ref[rows, 512:]
            out_ref[rows, 512:] = with_squares(came + held, squares_of(came) + squares_of(held)).astype(BF16)
            return 0

        lax.fori_loop(0, HALF // 16, add, 0)


def to_lanes(column):
    n = column.shape[0]
    same = lax.broadcasted_iota(jnp.int32, (n, 128), 0) == lane_of((n, 128))
    return jnp.sum(jnp.where(same, column, 0.0), axis=0, keepdims=True)


def to_column(row, n=128):
    same = lax.broadcasted_iota(jnp.int32, (n, 128), 0) == lane_of((n, 128))
    return jnp.sum(jnp.where(same, row, 0.0), axis=1, keepdims=True)


def total_kernel(d_ref, base_ref, own_ref, up2_ref, up3_ref, down2_ref, down3_ref, ids_ref, logits_ref, out_ref, ids_col, lse_col, picked_col):
    shift = lax.rem(WIDE - (OWN - STEP) * d_ref[0], WIDE)
    for begin in range(0, ROWS, 128):
        n = min(128, ROWS - begin)
        row = ids_ref[:, begin : begin + n]
        same = lax.broadcasted_iota(jnp.int32, (n, n), 0) == lane_of((n, n))
        ids_col[begin : begin + n, :] = jnp.sum(jnp.where(same, row.astype(F32), 0.0), axis=1, keepdims=True)
    for start, left_ref, right_ref in ((0, up3_ref, down2_ref), (HALF, up2_ref, down3_ref)):

        def finish(i, _):
            part = pl.ds(pl.multiple_of(i * 16, 16), 16)
            rows = pl.ds(pl.multiple_of(start + i * 16, 16), 16)
            own, left, right = own_ref[rows, :], left_ref[part, :].astype(F32), right_ref[part, :].astype(F32)
            squares = squares_of(own[:, 512:]) + (squares_of(left[:, 512:]) + squares_of(right[:, 512:]))
            scale = lax.rsqrt(squares / D + EPSILON)
            logits = pltpu.roll((own + (left + right)) * scale, shift, 1)
            lane = lane_of(logits.shape)
            logits_ref[rows, :] = logits
            kept = jnp.where(lane < OWN, logits, -jnp.inf)
            top = jnp.max(kept, axis=1, keepdims=True)
            lse_col[rows, :] = top + jnp.log(jnp.sum(jnp.exp(kept - top), axis=1, keepdims=True))
            target = ids_col[rows, :].astype(jnp.int32) - base_ref[0]
            hit = (lane == target) & (lane < OWN)
            picked_col[rows, :] = jnp.sum(jnp.where(hit, logits, 0.0), axis=1, keepdims=True)
            return 0

        lax.fori_loop(0, HALF // 16, finish, 0)
    out_ref[...] = jnp.zeros(out_ref.shape, F32)
    for k, begin in enumerate(range(0, ROWS, 128)):
        n = min(128, ROWS - begin)
        for place, col in ((k, lse_col), (8 + k, picked_col)):
            row = to_lanes(col[begin : begin + n, :])
            out_ref[:, place : place + 1, :] = jnp.broadcast_to(row[None], (out_ref.shape[0], 1, 128))


def joined(parts_ref):
    lse = parts_ref[:, 0:8, :]
    top = jnp.max(lse, axis=0)
    return top + jnp.log(jnp.sum(jnp.exp(lse - top[None]), axis=0)), jnp.sum(parts_ref[:, 8:16, :], axis=0)


def join_kernel(parts_ref, out_ref):
    lse, picked = joined(parts_ref)
    out_ref[:, 0:8, :] = jnp.broadcast_to(lse[None], (out_ref.shape[0], 8, 128))
    out_ref[:, 8:16, :] = jnp.broadcast_to(picked[None], (out_ref.shape[0], 8, 128))


def last_kernel(d_ref, logits_ref, parts_ref, out_ref, target_ref, lse_col, target_col):
    lse, picked = joined(parts_ref)
    for k, begin in enumerate(range(0, ROWS, 128)):
        n = min(128, ROWS - begin)
        lse_col[begin : begin + n, :] = to_column(lse[k : k + 1, :], n)
        target_col[begin : begin + n, :] = to_column(picked[k : k + 1, :] - lse[k : k + 1, :], n)

    def write(i, _):
        rows = pl.ds(pl.multiple_of(i * 16, 16), 16)
        out_ref[rows, :] = (logits_ref[rows, :] - lse_col[rows, :])[:, :OWN].astype(BF16)
        return 0

    lax.fori_loop(0, ROWS // 16, write, 0)
    own = ROWS // DP
    first = pl.multiple_of(d_ref[0] * own, 8)
    target_ref[:, 0:128] = to_lanes(target_col[pl.ds(first, 128), :])
    target_ref[:, 128:own] = to_lanes(target_col[pl.ds(first + 128, own - 128), :])[:, : own - 128]


def shape(*dims, dtype=F32):
    return jax.ShapeDtypeStruct(dims, dtype)


def cost(flops, nbytes):
    return pl.CostEstimate(flops=flops, bytes_accessed=nbytes, transcendentals=0)


def body(hidden_states, norm_gain, lm_head, target_ids):
    width = hidden_states.shape[1]
    d = lax.axis_index("dp")
    group = lax.axis_index("section") * lax.axis_size("tp") + lax.axis_index("tp")
    dp = d.astype(jnp.int32).reshape(1)
    base = ((group * DP + d) * OWN).astype(jnp.int32).reshape(1)
    weights = lm_head.T
    gain = norm_gain.reshape(1, width)
    ids = target_ids.reshape(1, ROWS)

    def chunk(offsets):
        def at(j, d_ref):
            offset = offsets[-1]
            for k, value in enumerate(offsets[:-1]):
                offset = jnp.where(j == k, value, offset)
            return lax.rem(d_ref[0] + offset, DP)

        return [
            pl.BlockSpec((STEP, width), lambda j, d_ref: (at(j, d_ref), 0)),
            pl.BlockSpec((TAIL, width), lambda j, d_ref: ((at(j, d_ref) + 1) * (STEP // TAIL), 0)),
        ]

    def fixed(*dims):
        return pl.BlockSpec(dims, lambda j, d_ref: (0, 0))

    hg, sq, up1, down1 = pl.pallas_call(
        first_kernel,
        grid_spec=pltpu.PrefetchScalarGridSpec(
            num_scalar_prefetch=1,
            grid=(2,),
            in_specs=[pl.BlockSpec((HALF, width), lambda j, d_ref: (j, 0)), fixed(1, width)] + chunk((2,)),
            out_specs=[
                pl.BlockSpec((HALF, width), lambda j, d_ref: (j, 0)),
                pl.BlockSpec((HALF, 128), lambda j, d_ref: (j, 0)),
                fixed(HALF, WIDE),
                fixed(HALF, WIDE),
            ],
        ),
        out_shape=(
            shape(ROWS, width, dtype=BF16),
            shape(ROWS, 128),
            shape(HALF, WIDE, dtype=BF16),
            shape(HALF, WIDE, dtype=BF16),
        ),
        compiler_params=VMEM,
        cost_estimate=cost(2 * ROWS * WIDE * width, 9_000_000),
        name="first_window",
    )(dp, hidden_states, gain, weights, weights)

    up = [(i, (i + 1) % DP) for i in range(DP)]
    down = [(i, (i - 1) % DP) for i in range(DP)]
    up1_in = lax.ppermute(up1, "dp", up)
    down1_in = lax.ppermute(down1, "dp", down)

    up2, up_held, down2, down_held, own = pl.pallas_call(
        rest_kernel,
        grid_spec=pltpu.PrefetchScalarGridSpec(
            num_scalar_prefetch=1,
            grid=(3,),
            in_specs=[fixed(ROWS, width), fixed(ROWS, 128)] + chunk((1, 3, 0)),
            out_specs=[fixed(HALF, WIDE)] * 4 + [fixed(ROWS, WIDE)],
            scratch_shapes=[pltpu.VMEM((ROWS, WIDE), F32)],
        ),
        out_shape=(
            shape(HALF, WIDE, dtype=BF16),
            shape(HALF, WIDE),
            shape(HALF, WIDE, dtype=BF16),
            shape(HALF, WIDE),
            shape(ROWS, WIDE),
        ),
        compiler_params=VMEM,
        cost_estimate=cost(6 * ROWS * WIDE * width, 16_000_000),
        name="other_windows",
    )(dp, hg, sq, weights, weights)
    up2_in = lax.ppermute(up2, "dp", up)
    down2_in = lax.ppermute(down2, "dp", down)

    up3, down3 = pl.pallas_call(
        add_kernel,
        in_specs=[whole()] * 4,
        out_specs=[whole()] * 2,
        out_shape=(shape(HALF, WIDE, dtype=BF16), shape(HALF, WIDE, dtype=BF16)),
        compiler_params=VMEM,
        cost_estimate=cost(ROWS * WIDE, 3_500_000),
        name="add_passing",
    )(up1_in, up_held, down1_in, down_held)
    up3_in = lax.ppermute(up3, "dp", up)
    down3_in = lax.ppermute(down3, "dp", down)

    scalar = pl.BlockSpec(memory_space=pltpu.SMEM)
    near = lax.axis_size(("section", "dp"))
    logits, parts = pl.pallas_call(
        total_kernel,
        in_specs=[scalar, scalar] + [whole()] * 6,
        out_specs=[whole()] * 2,
        out_shape=(shape(ROWS, WIDE), shape(near, 16, 128)),
        scratch_shapes=[pltpu.VMEM((ROWS, 1), F32)] * 3,
        compiler_params=VMEM,
        name="row_totals",
    )(dp, base, own, up2_in, up3_in, down2_in, down3_in, ids)
    parts = lax.all_to_all(parts, ("section", "dp"), 0, 0, tiled=True)
    parts = pl.pallas_call(
        join_kernel,
        in_specs=[whole()],
        out_specs=whole(),
        out_shape=shape(lax.axis_size("tp"), 16, 128),
        compiler_params=VMEM,
        name="join_totals",
    )(parts)
    parts = lax.all_to_all(parts, "tp", 0, 0, tiled=True)
    logprobs, target = pl.pallas_call(
        last_kernel,
        in_specs=[scalar, whole(), whole()],
        out_specs=[whole()] * 2,
        out_shape=(shape(ROWS, OWN, dtype=BF16), shape(1, ROWS // DP)),
        scratch_shapes=[pltpu.VMEM((ROWS, 1), F32)] * 2,
        compiler_params=VMEM,
        name="log_probabilities",
    )(dp, logits, parts)
    return logprobs, target.reshape(ROWS // DP)


def solution(mesh):
    placed = (P(None, "dp"), P("dp"), P("dp", ("section", "tp")), P())
    return jax.shard_map(
        body,
        mesh=mesh,
        in_specs=placed,
        out_specs=(P(None, ("section", "tp", "dp")), P("dp")),
        check_vma=False,
    )
```

time: 384 us -> 103 us (0.27)
  blocking collectives: 277 us -> 34.8 us
  waiting for transfers between devices: 70.7 us -> 10.5 us
  Pallas kernels: 0 us -> 46 us
  between operations: 14.1 us -> 0.69 us
  matrix products: 11.7 us -> 0 us
  starting transfers between devices: 0.04 us -> 8.97 us
  other arithmetic: 7.08 us -> 0 us
    psum x2 -> x0, blocking collectives: 138 us -> none  [the longest x1 128 us: body(): lax.psum((jnp.sum(jnp.exp(logits - row_top[:, None]), axis=1), picked), (...]
    pmax x1 -> x0, blocking collectives: 125 us -> none  [body(): row_top = lax.pmax(jnp.max(logits, axis=1), ('section', 'tp'))]
    unnamed x2 -> x0, waiting for transfers between devices: 70.7 us -> none
    pallas_call x0 -> x6, Pallas kernels: none -> 46 us  [the longest x1 17.3 us: body(): pl.pallas_call(total_kernel, in_specs=[scalar, scalar] + [whole()] * 6, o...]
    all_to_all x1 -> x2, blocking collectives: 14.8 us -> 34.8 us  [the longest x1 21.2 us: body(): parts = lax.all_to_all(parts, 'tp', 0, 0, tiled=True)]
    dot_general x1 -> x0, matrix products: 11.7 us -> none  [body(): jnp.dot(normed, lm_head, preferred_element_type=jnp.float32)]
    ppermute x0 -> x6, waiting for transfers between devices: none -> 10.5 us  [the longest x1 10.2 us: body(): up3_in = lax.ppermute(up3, 'dp', up)]
    ppermute x0 -> x6, starting transfers between devices: none -> 8.97 us  [the longest x1 2.66 us: body(): down3_in = lax.ppermute(down3, 'dp', down)]
  transfers between devices with their start and end apart: 1 -> 6, of which waited for: 1 -> 2; matrix products, arithmetic and copies ran while one was open for 0% -> 0% of each run, Pallas kernels for 0% -> 15%
where the time goes in v1:
time: 103 us
  Pallas kernels  46 us (45%)
  blocking collectives  34.8 us (34%)
  waiting for transfers between devices  10.5 us (10%)
  starting transfers between devices  8.97 us (9%)
  local copies, waits for them, and re-layouts  2.23 us (2%)
    all_to_all x1, blocking collectives, body(): parts = lax.all_to_all(parts, 'tp', 0, 0, tiled=True)  21.2 us
    pallas_call x1, Pallas kernels, body(): pl.pallas_call(total_kernel, in_specs=[scalar, scalar] + [whole()] * 6, o...  17.3 us
    all_to_all x1, blocking collectives, body(): parts = lax.all_to_all(parts, ('section', 'dp'), 0, 0, tiled=True)  13.5 us
    pallas_call x1, Pallas kernels, body(): pl.pallas_call(rest_kernel, grid_spec=pltpu.PrefetchScalarGridSpec(num_sc...  11.1 us
    ppermute x1, waiting for transfers between devices, body(): up3_in = lax.ppermute(up3, 'dp', up)  10.2 us
    pallas_call x1, Pallas kernels, body(): pl.pallas_call(first_kernel, grid_spec=pltpu.PrefetchScalarGridSpec(num_s...  9.26 us
    pallas_call x1, Pallas kernels, body(): pl.pallas_call(last_kernel, in_specs=[scalar, whole(), whole()], out_spec...  4.31 us
    pallas_call x1, Pallas kernels, body(): pl.pallas_call(add_kernel, in_specs=[whole()] * 4, out_specs=[whole()] *...  3.92 us
  transfers between devices with their start and end apart: 6, of which 2 were waited for; matrix products, arithmetic and copies ran while one was open for 0% of the time, Pallas kernels for 15%

profile of v1, /device:TPU:1, one launch (start us, length us, event | category | flops | bytes accessed | tf_op | source)
XLA Modules:
  0.0 103.1 jit_solution(5581105017908815329)
XLA Ops:
  0.6 0.0 copy-start.1
  0.6 0.7 copy-done.1
  1.3 9.3 %first_window.1 = (bf16[672,2048]{1,0:T(8,128)(2,1)S(1)}, f32[672,128]{1,0:T(8,128)S(1)}, bf16[336,640]{1,0:T(8,128)(2,1)S(1)}, bf16[336,640]{1,0:T(8,128)(2,1)S(1)}) custom-call(s32[1]{0:T(128)} %bitcast.d_ref, bf16[672,2048]{1,0:T(8,128)(2,1)} %x_ref.1, f32[1,2048]{1,0:T(1,128)S(1)} %bitcast.5, bf16[2376,2048]{1,0:T(8,128)(2,1)} %bitcast.6, ...), custom_call_target="tpu_custom_call" | custom-call | flops 1761607680 | bytes 9000000 | tf_op jit(solution)/shard_map/first_window/pallas_call | solution.py:231
  10.6 0.0 copy-start
  10.6 1.5 %copy-done = bf16[672,2048]{1,0:T(8,128)(2,1)} copy-done((bf16[672,2048]{1,0:T(8,128)(2,1)}, bf16[672,2048]{1,0:T(8,128)(2,1)S(1)}, u32[]{:S(2)}) %copy-start) | copy-done | bytes 2752536
  12.1 2.1 %collective-permute-start.1 = (bf16[336,640]{1,0:T(8,128)(2,1)S(1)}, bf16[336,640]{1,0:T(8,128)(2,1)S(1)}, u32[]{:S(2)}, u32[]{:S(2)}) collective-permute-start(bf16[336,640]{1,0:T(8,128)(2,1)S(1)} %get-tuple-element.21), channel_id=1, source_target_pairs={{0,1},{1,2},{2,3},{3,0},{4,5},{5,6},{6,7},{7,4},{8,9},{9,10},{10,1... | collective-permute-start | bytes 1290248 | tf_op jit(solution)/shard_map/ppermute | solution.py:257
  14.3 1.4 %collective-permute-start.2 = (bf16[336,640]{1,0:T(8,128)(2,1)S(1)}, bf16[336,640]{1,0:T(8,128)(2,1)S(1)}, u32[]{:S(2)}, u32[]{:S(2)}) collective-permute-start(bf16[336,640]{1,0:T(8,128)(2,1)S(1)} %get-tuple-element.23), channel_id=1, source_target_pairs={{0,3},{1,0},{2,1},{3,2},{4,7},{5,4},{6,5},{7,6},{8,11},{9,8},{10,9... | collective-permute-start | bytes 1290248 | tf_op jit(solution)/shard_map/ppermute | solution.py:258
  15.7 0.0 copy-start.2
  15.7 11.1 %other_windows.1 = (bf16[336,640]{1,0:T(8,128)(2,1)S(1)}, f32[336,640]{1,0:T(8,128)S(1)}, bf16[336,640]{1,0:T(8,128)(2,1)S(1)}, f32[336,640]{1,0:T(8,128)S(1)}, f32[672,640]{1,0:T(8,128)}) custom-call(s32[1]{0:T(128)} %bitcast.d_ref, bf16[672,2048]{1,0:T(8,128)(2,1)} %copy-done, f32[672,128]{1,0:T(8,128)S(1)} %get-tuple-element.18.sq_ref, ...), custom_call_target="tpu_custom_call" | custom-call | flops 5284823040 | bytes 16000000 | tf_op jit(solution)/shard_map/other_windows/pallas_call | solution.py:260
  26.8 0.0 collective-permute-start
  26.9 2.7 %collective-permute-start.4 = (bf16[336,640]{1,0:T(8,128)(2,1)S(1)}, bf16[336,640]{1,0:T(8,128)(2,1)S(1)}, u32[]{:S(2)}, u32[]{:S(2)}) collective-permute-start(bf16[336,640]{1,0:T(8,128)(2,1)S(1)} %get-tuple-element.26), channel_id=1, source_target_pairs={{0,3},{1,0},{2,1},{3,2},{4,7},{5,4},{6,5},{7,6},{8,11},{9,8},{10,9... | collective-permute-start | bytes 1290248 | tf_op jit(solution)/shard_map/ppermute | solution.py:281
  29.5 0.0 collective-permute-done.1.up_in_ref
  29.5 0.0 collective-permute-done.2.down_in_ref
  29.5 3.9 %add_passing.1 = (bf16[336,640]{1,0:T(8,128)(2,1)S(1)}, bf16[336,640]{1,0:T(8,128)(2,1)S(1)}) custom-call(bf16[336,640]{1,0:T(8,128)(2,1)S(1)} %collective-permute-done.1.up_in_ref, f32[336,640]{1,0:T(8,128)S(1)} %get-tuple-element.22.up_held_ref, bf16[336,640]{1,0:T(8,128)(2,1)S(1)} %collective-permute-done.2.down_in_ref, ...), custom_call_target="tpu_custom_call" | custom-call | flops 430080 | bytes 3500000 | tf_op jit(solution)/shard_map/add_passing/pallas_call | solution.py:283
  33.4 0.1 collective-permute-start.3
  33.5 2.7 %collective-permute-start.5 = (bf16[336,640]{1,0:T(8,128)(2,1)S(1)}, bf16[336,640]{1,0:T(8,128)(2,1)S(1)}, u32[]{:S(2)}, u32[]{:S(2)}) collective-permute-start(bf16[336,640]{1,0:T(8,128)(2,1)S(1)} %get-tuple-element.27), channel_id=1, source_target_pairs={{0,3},{1,0},{2,1},{3,2},{4,7},{5,4},{6,5},{7,6},{8,11},{9,8},{10,9... | collective-permute-start | bytes 1290248 | tf_op jit(solution)/shard_map/ppermute | solution.py:293
  36.2 0.0 copy-done.2
  36.2 0.3 collective-permute-done.up2_ref
  36.5 0.0 collective-permute-done.4.down2_ref
  36.5 10.2 %collective-permute-done.3.up3_ref = bf16[336,640]{1,0:T(8,128)(2,1)S(1)} collective-permute-done((bf16[336,640]{1,0:T(8,128)(2,1)S(1)}, bf16[336,640]{1,0:T(8,128)(2,1)S(1)}, u32[]{:S(2)}, u32[]{:S(2)}) %collective-permute-start.3) | collective-permute-done | bytes 430112 | tf_op jit(solution)/shard_map/ppermute | solution.py:292
  46.7 0.0 collective-permute-done.5.down3_ref
  46.7 17.3 %row_totals.1 = (f32[672,640]{1,0:T(8,128)S(1)}, f32[16,16,128]{2,1,0:T(8,128)S(1)}) custom-call(s32[1]{0:T(128)} %bitcast.d_ref, s32[1]{0:T(128)} %bitcast.1.base_ref, f32[672,640]{1,0:T(8,128)} %get-tuple-element.19.own_ref, bf16[336,640]{1,0:T(8,128)(2,1)S(1)} %collective-permute-done.up2_ref, bf16[336,640]{1,0:T(8,128)(2,1)S(1)} %collective-permute-done.3.up3_ref, ...), custom_call_target="tpu_custom_call" | custom-call | tf_op jit(solution)/shard_map/row_totals/pallas_call | solution.py:297
  64.0 13.5 %all_to_all.10.parts_ref = f32[16,16,128]{2,1,0:T(8,128)S(1)} all-to-all(f32[16,16,128]{2,1,0:T(8,128)S(1)} %get-tuple-element.29), channel_id=1, replica_groups=mesh['section'=4,'tp'=16,'dp'=4] {'section','dp'}, dimensions={0} | all-to-all | bytes 262144 | tf_op jit(solution)/shard_map/all_to_all | solution.py:306
  77.6 21.2 %all_to_all.11.parts_ref = f32[16,16,128]{2,1,0:T(8,128)S(1)} all-to-all(f32[16,16,128]{2,1,0:T(8,128)S(1)} %join_totals.1), channel_id=1, replica_groups=mesh['section'=4,'tp'=16,'dp'=4] {'tp'}, dimensions={0} | all-to-all | bytes 262144 | tf_op jit(solution)/shard_map/all_to_all | solution.py:315
  98.8 4.3 %log_probabilities.1 = (bf16[672,594]{1,0:T(8,128)(2,1)}, f32[1,168]{1,0:T(1,128)}) custom-call(s32[1]{0:T(128)} %bitcast.d_ref, f32[672,640]{1,0:T(8,128)S(1)} %get-tuple-element.28.logits_ref, f32[16,16,128]{2,1,0:T(8,128)S(1)} %all_to_all.11.parts_ref), custom_call_target="tpu_custom_call" | custom-call | tf_op jit(solution)/shard_map/log_probabilities/pallas_call | solution.py:316
  (2 shorter events, 0.0 us)
Async XLA Ops:
  0.6 0.7 copy-start.1
  10.6 1.5 %copy-start = (bf16[672,2048]{1,0:T(8,128)(2,1)}, bf16[672,2048]{1,0:T(8,128)(2,1)S(1)}, u32[]{:S(2)}) copy-start(bf16[672,2048]{1,0:T(8,128)(2,1)S(1)} %get-tuple-element.17.hg_ref) | copy-start | bytes 8257540
  12.1 17.4 %collective-permute-start.1 = (bf16[336,640]{1,0:T(8,128)(2,1)S(1)}, bf16[336,640]{1,0:T(8,128)(2,1)S(1)}, u32[]{:S(2)}, u32[]{:S(2)}) collective-permute-start(bf16[336,640]{1,0:T(8,128)(2,1)S(1)} %get-tuple-element.21), channel_id=1, source_target_pairs={{0,1},{1,2},{2,3},{3,0},{4,5},{5,6},{6,7},{7,4},{8,9},{9,10},{10,1... | collective-permute-start | bytes 1290248 | tf_op jit(solution)/shard_map/ppermute | solution.py:257
  14.3 15.3 %collective-permute-start.2 = (bf16[336,640]{1,0:T(8,128)(2,1)S(1)}, bf16[336,640]{1,0:T(8,128)(2,1)S(1)}, u32[]{:S(2)}, u32[]{:S(2)}) collective-permute-start(bf16[336,640]{1,0:T(8,128)(2,1)S(1)} %get-tuple-element.23), channel_id=1, source_target_pairs={{0,3},{1,0},{2,1},{3,2},{4,7},{5,4},{6,5},{7,6},{8,11},{9,8},{10,9... | collective-permute-start | bytes 1290248 | tf_op jit(solution)/shard_map/ppermute | solution.py:258
  15.7 20.5 %copy-start.2 = (s32[672]{0:T(1024)S(1)}, s32[672]{0:T(1024)}, u32[]{:S(2)}) copy-start(s32[672]{0:T(1024)} %param.7) | copy-start | bytes 8068
  26.8 9.7 %collective-permute-start = (bf16[336,640]{1,0:T(8,128)(2,1)S(1)}, bf16[336,640]{1,0:T(8,128)(2,1)S(1)}, u32[]{:S(2)}, u32[]{:S(2)}) collective-permute-start(bf16[336,640]{1,0:T(8,128)(2,1)S(1)} %get-tuple-element.20), channel_id=1, source_target_pairs={{0,1},{1,2},{2,3},{3,0},{4,5},{5,6},{6,7},{7,4},{8,9},{9,10},{10,1... | collective-permute-start | bytes 1290248 | tf_op jit(solution)/shard_map/ppermute | solution.py:280
  26.9 9.7 %collective-permute-start.4 = (bf16[336,640]{1,0:T(8,128)(2,1)S(1)}, bf16[336,640]{1,0:T(8,128)(2,1)S(1)}, u32[]{:S(2)}, u32[]{:S(2)}) collective-permute-start(bf16[336,640]{1,0:T(8,128)(2,1)S(1)} %get-tuple-element.26), channel_id=1, source_target_pairs={{0,3},{1,0},{2,1},{3,2},{4,7},{5,4},{6,5},{7,6},{8,11},{9,8},{10,9... | collective-permute-start | bytes 1290248 | tf_op jit(solution)/shard_map/ppermute | solution.py:281
  33.4 13.3 %collective-permute-start.3 = (bf16[336,640]{1,0:T(8,128)(2,1)S(1)}, bf16[336,640]{1,0:T(8,128)(2,1)S(1)}, u32[]{:S(2)}, u32[]{:S(2)}) collective-permute-start(bf16[336,640]{1,0:T(8,128)(2,1)S(1)} %get-tuple-element.25), channel_id=1, source_target_pairs={{0,1},{1,2},{2,3},{3,0},{4,5},{5,6},{6,7},{7,4},{8,9},{9,10},{10,1... | collective-permute-start | bytes 1290248 | tf_op jit(solution)/shard_map/ppermute | solution.py:292
  33.5 13.2 %collective-permute-start.5 = (bf16[336,640]{1,0:T(8,128)(2,1)S(1)}, bf16[336,640]{1,0:T(8,128)(2,1)S(1)}, u32[]{:S(2)}, u32[]{:S(2)}) collective-permute-start(bf16[336,640]{1,0:T(8,128)(2,1)S(1)} %get-tuple-element.27), channel_id=1, source_target_pairs={{0,3},{1,0},{2,1},{3,2},{4,7},{5,4},{6,5},{7,6},{8,11},{9,8},{10,9... | collective-permute-start | bytes 1290248 | tf_op jit(solution)/shard_map/ppermute | solution.py:293

commit v2 on v0

v2 whole, which is shorter than its diff:
```python
import jax
import jax.numpy as jnp
from jax import lax
from jax.experimental import pallas as pl
from jax.experimental.pallas import tpu as pltpu
from jax.sharding import PartitionSpec as P

D = 8192
EPSILON = 1e-06
ROWS = 672
HALF = ROWS // 2
DP = 4
OWN = 594
STEP = 592
SPAN = 600
WIDE = 640
LAST = 512
BLOCK = 112
PIECE = 48
F32 = jnp.float32
BF16 = jnp.bfloat16
CONTRACT = (((1,), (1,)), ((), ()))


def whole():
    return pl.BlockSpec(memory_space=pltpu.VMEM)


def far():
    return pl.BlockSpec(memory_space=pltpu.HBM)


def vmem(mib):
    return pltpu.CompilerParams(vmem_limit_bytes=mib * 1024 * 1024)


def shape(*dims, dtype=F32):
    return jax.ShapeDtypeStruct(dims, dtype)


def cost(flops, nbytes):
    return pl.CostEstimate(flops=flops, bytes_accessed=nbytes, transcendentals=0)


def lane_of(dims):
    return lax.broadcasted_iota(jnp.int32, dims, 1)


def row_of(dims):
    return lax.broadcasted_iota(jnp.int32, dims, 0)


def to_lanes(column):
    dims = (column.shape[0], 128)
    return jnp.sum(jnp.where(row_of(dims) == lane_of(dims), column, 0.0), axis=0, keepdims=True)


def to_column(row, n=128):
    return jnp.sum(jnp.where(row_of((n, 128)) == lane_of((n, 128)), row, 0.0), axis=1, keepdims=True)


def lane_groups():
    return [(k, begin, min(128, ROWS - begin)) for k, begin in enumerate(range(0, ROWS, 128))]


def window_copy(w_ref, chunk, held_ref, sem):
    rows = pl.ds(pl.multiple_of(lax.rem(chunk, DP) * STEP, 16), SPAN)
    return pltpu.make_async_copy(w_ref.at[rows], held_ref.at[pl.ds(0, SPAN)], sem)


def dot(left, right):
    return lax.dot_general(left, right, CONTRACT, preferred_element_type=F32)


def with_squares(tile, total, place):
    lane = lane_of(tile.shape)
    high = total.astype(BF16).astype(F32)
    middle = (total - high).astype(BF16).astype(F32)
    terms = jnp.where(lane == place, high, jnp.where(lane == place + 1, middle, total - high - middle))
    return jnp.where(lane < place, tile, jnp.where(lane < place + 3, terms, 0.0))


def squares_of(tile, place):
    lane = lane_of(tile.shape)
    return jnp.sum(jnp.where((lane >= place) & (lane < place + 3), tile, 0.0), axis=1, keepdims=True)


def scaled(x, g_ref, hg_ref, sq_ref, at):
    for begin in range(at, at + HALF, PIECE):
        rows = slice(begin, begin + PIECE)
        total = jnp.zeros((PIECE, 128), F32)
        for k in range(0, x.shape[1], 128):
            part = x[rows, k : k + 128].astype(F32)
            hg_ref[rows, k : k + 128] = (part * g_ref[:, k : k + 128]).astype(BF16)
            total = total + part * part
        sq_ref[rows, :] = jnp.broadcast_to(jnp.sum(total, axis=1, keepdims=True), (PIECE, 128))


def put_window(out_ref, product, squares, place):
    out_ref[:, :LAST] = product[:, :LAST].astype(BF16)
    out_ref[:, LAST:] = with_squares(product[:, LAST:], squares, place).astype(BF16)


def first_kernel(x_ref, g_ref, w_ref, hg_ref, sq_ref, up_ref, down_ref, w_up_ref, w_down_ref, x_held, g_held, w_held, sem):
    g_copy = pltpu.make_async_copy(g_ref, g_held, sem.at[0])
    w_copy = window_copy(w_ref, lax.axis_index("dp") + 2, w_held, sem.at[1])
    later = [window_copy(w_ref, lax.axis_index("dp") + 1, w_up_ref, sem.at[2]), window_copy(w_ref, lax.axis_index("dp") + 3, w_down_ref, sem.at[5])]
    x_copies = []
    for half in (0, 1):
        rows = pl.ds(half * HALF, HALF)
        x_copies.append(pltpu.make_async_copy(x_ref.at[rows], x_held.at[rows], sem.at[3 + half]))
    for copy in [g_copy, x_copies[0], w_copy, x_copies[1]] + later:
        copy.start()
    g_copy.wait()
    x_copies[0].wait()
    scaled(x_held, g_held, hg_ref, sq_ref, 0)
    w_copy.wait()
    x_copies[1].wait()
    for half, out_ref in ((0, up_ref), (1, down_ref)):
        rows = slice(half * HALF, half * HALF + HALF)
        if half == 1:
            scaled(x_held, g_held, hg_ref, sq_ref, HALF)
        put_window(out_ref, dot(hg_ref[rows, :], w_held[...]), sq_ref[rows, :], SPAN - LAST)
    for copy in later:
        copy.wait()


def direct_kernel(hg_ref, sq_ref, w_up_ref, w_down_ref, up_ref, down_ref):
    for i, (held_ref, out_ref) in enumerate(((w_up_ref, up_ref), (w_down_ref, down_ref))):
        rows = slice(HALF - i * HALF, ROWS - i * HALF)
        shift = lax.rem(WIDE - (OWN - STEP) * lax.rem(lax.axis_index("dp") + 1 + 2 * i, DP), WIDE)
        product = pltpu.roll(dot(hg_ref[rows, :], held_ref[...]), shift, 1)
        put_window(out_ref, product, sq_ref[rows, :], OWN - LAST)


def passing_kernel(hg_ref, sq_ref, w_up_ref, w_down_ref, up_in_ref, down_in_ref, up_ref, down_ref):
    for i, (held_ref, in_ref, out_ref) in enumerate(((w_up_ref, up_in_ref, up_ref), (w_down_ref, down_in_ref, down_ref))):
        rows = slice(i * HALF, i * HALF + HALF)
        shift = lax.rem(WIDE - (OWN - STEP) * lax.rem(lax.axis_index("dp") + 1 + 2 * i, DP), WIDE)
        came = in_ref[...].astype(F32)
        total = sq_ref[rows, :] + squares_of(came[:, LAST:], SPAN - LAST)
        product = pltpu.roll(dot(hg_ref[rows, :], held_ref[...]) + came, shift, 1)
        put_window(out_ref, product, total, OWN - LAST)


def own_kernel(hg_ref, w_ref, own_ref, w_held, sem):
    copy = window_copy(w_ref, lax.axis_index("dp"), w_held, sem.at[0])
    copy.start()
    copy.wait()
    own_ref[...] = dot(hg_ref[...], w_held[...])


def part_kernel(ids_ref, sq_ref, own_ref, up_ref, down_ref, sum_ref, part_ref, target_ref):
    group = lax.axis_index("section") * lax.axis_size("tp") + lax.axis_index("tp")
    base = (group * DP + lax.axis_index("dp")) * OWN
    shift = lax.rem(WIDE - (OWN - STEP) * lax.axis_index("dp"), WIDE)
    for k, begin, n in lane_groups():
        same = row_of((n, n)) == lane_of((n, n))
        ids = jnp.sum(jnp.where(same, ids_ref[:, begin : begin + n].astype(F32), 0.0), axis=1, keepdims=True)
        target = ids.astype(jnp.int32) - base
        target_ref[begin : begin + n, :] = jnp.broadcast_to(jnp.where(target < OWN, target, -1), (n, 128))
    for begin in range(0, ROWS, BLOCK):
        rows = slice(begin, begin + BLOCK)
        part = slice(begin % HALF, begin % HALF + BLOCK)
        came = (down_ref if begin < HALF else up_ref)[part, :].astype(F32)
        sum_ref[rows, :] = pltpu.roll(own_ref[rows, :], shift, 1) + came
        part_ref[rows, :] = sq_ref[rows, :] + squares_of(came[:, LAST:], OWN - LAST)


def put_rows(out_ref, place, row):
    out_ref[:, place : place + 1, :] = jnp.broadcast_to(row[None], (out_ref.shape[0], 1, 128))


def total_kernel(sum_ref, part_ref, target_ref, up_ref, down_ref, logits_ref, out_ref, lse_col, picked_col):
    lane = lane_of((PIECE, 128))
    for begin in range(0, ROWS, PIECE):
        rows = slice(begin, begin + PIECE)
        part = slice(begin % HALF, begin % HALF + PIECE)
        came_ref = up_ref if begin < HALF else down_ref
        squares = part_ref[rows, :] + squares_of(came_ref[part, LAST:].astype(F32), OWN - LAST)
        scale, target = lax.rsqrt(squares / D + EPSILON), target_ref[rows, :]
        tiles = []
        for k in range(0, WIDE, 128):
            tile = (sum_ref[rows, k : k + 128] + came_ref[part, k : k + 128].astype(F32)) * scale
            logits_ref[rows, k : k + 128] = tile
            tiles.append(jnp.where(lane < OWN - k, tile, -jnp.inf) if k + 128 > OWN else tile)
        top = tiles[0]
        for tile in tiles[1:]:
            top = jnp.maximum(top, tile)
        top = jnp.max(top, axis=1, keepdims=True)
        total = picked = jnp.zeros((PIECE, 128), F32)
        for k, tile in enumerate(tiles):
            total = total + jnp.exp(tile - top)
            picked = picked + jnp.where(lane == target - 128 * k, tile, 0.0)
        lse_col[rows, :] = top + jnp.log(jnp.sum(total, axis=1, keepdims=True))
        picked_col[rows, :] = jnp.sum(picked, axis=1, keepdims=True)
    for k, begin, n in lane_groups():
        put_rows(out_ref, k, to_lanes(lse_col[begin : begin + n, :]))
    own = ROWS // DP
    for k in range(DP):
        for place, begin, n in ((6, k * own, 128), (7, k * own + 128, own - 128)):
            row = to_lanes(picked_col[begin : begin + n, :])
            for part in range(k, out_ref.shape[0], DP):
                out_ref[part, place : place + 1, :] = row


def joined(parts_ref):
    parts = parts_ref[...]
    top = jnp.max(parts, axis=0)
    return top + jnp.log(jnp.sum(jnp.exp(parts - top[None]), axis=0)), jnp.sum(parts, axis=0)


def join_kernel(parts_ref, out_ref):
    lse, picked = joined(parts_ref)
    both = jnp.where(row_of(lse.shape) < 6, lse, picked)
    out_ref[...] = jnp.broadcast_to(both[None], out_ref.shape)


def last_kernel(logits_ref, parts_ref, out_ref, target_ref, out_held, lse_col, out_sem):
    lse, picked = joined(parts_ref)
    copies = []
    for k, begin, n in lane_groups():
        rows = slice(begin, begin + n)
        column = to_column(lse[k : k + 1, :], n)
        lse_col[rows, :] = column
        out_held[rows, :] = (logits_ref[rows, :] - column)[:, :OWN].astype(BF16)
        copies.append(pltpu.make_async_copy(out_held.at[pl.ds(begin, n)], out_ref.at[pl.ds(begin, n)], out_sem.at[k]))
        copies[-1].start()
    own = ROWS // DP
    first = pl.multiple_of(lax.axis_index("dp") * own, 8)
    target_ref[:, 0:128] = picked[6:7, :] - to_lanes(lse_col[pl.ds(first, 128), :])
    target_ref[:, 128:own] = (picked[7:8, :] - to_lanes(lse_col[pl.ds(first + 128, own - 128), :]))[:, : own - 128]
    for copy in copies:
        copy.wait()


def body(hidden_states, norm_gain, lm_head, target_ids):
    width = hidden_states.shape[1]
    hidden_states = pltpu.with_memory_space_constraint(hidden_states, pltpu.HBM)
    weights = pltpu.with_memory_space_constraint(lm_head.T, pltpu.HBM)
    gain = pltpu.with_memory_space_constraint(norm_gain.reshape(1, width), pltpu.HBM)
    ids = target_ids.reshape(1, ROWS)
    sent = pltpu.VMEM((HALF, WIDE), BF16)
    window = pltpu.VMEM((WIDE, width), BF16)
    window_flops = 2 * ROWS * WIDE * width

    hg, sq, up1, down1, w_up, w_down = pl.pallas_call(
        first_kernel,
        in_specs=[far(), far(), far()],
        out_specs=[whole()] * 6,
        out_shape=(pltpu.VMEM((ROWS, width), BF16), pltpu.VMEM((ROWS, 128), F32), sent, sent, window, window),
        scratch_shapes=[
            pltpu.VMEM((ROWS, width), BF16),
            pltpu.VMEM((1, width), F32),
            window,
            pltpu.SemaphoreType.DMA((6,)),
        ],
        compiler_params=vmem(12),
        cost_estimate=cost(window_flops, 10_000_000),
        name="first_window",
    )(hidden_states, gain, weights)

    def shifted(array, k):
        return lax.ppermute(array, "dp", [(i, (i + k) % DP) for i in range(DP)])

    up1_in, down1_in = shifted(up1, 1), shifted(down1, -1)
    up2, down2 = pl.pallas_call(
        direct_kernel,
        in_specs=[whole()] * 4,
        out_specs=[whole()] * 2,
        out_shape=(sent, sent),
        compiler_params=vmem(8),
        cost_estimate=cost(window_flops, 10_000_000),
        name="direct_windows",
    )(hg, sq, w_up, w_down)
    up2_in, down2_in = shifted(up2, 1), shifted(down2, -1)
    up3, down3 = pl.pallas_call(
        passing_kernel,
        in_specs=[whole()] * 6,
        out_specs=[whole()] * 2,
        out_shape=(sent, sent),
        compiler_params=vmem(8),
        cost_estimate=cost(window_flops, 10_000_000),
        name="passing_windows",
    )(hg, sq, w_up, w_down, up1_in, down1_in)
    up3_in, down3_in = shifted(up3, 1), shifted(down3, -1)

    own = pl.pallas_call(
        own_kernel,
        in_specs=[whole(), far()],
        out_specs=whole(),
        out_shape=pltpu.VMEM((ROWS, WIDE), F32),
        scratch_shapes=[window, pltpu.SemaphoreType.DMA((1,))],
        compiler_params=vmem(8),
        cost_estimate=cost(window_flops, 6_000_000),
        name="own_window",
    )(hg, weights)
    sums, part, target = pl.pallas_call(
        part_kernel,
        in_specs=[whole()] * 5,
        out_specs=[whole()] * 3,
        out_shape=(pltpu.VMEM((ROWS, WIDE), F32), pltpu.VMEM((ROWS, 128), F32), pltpu.VMEM((ROWS, 128), jnp.int32)),
        compiler_params=vmem(10),
        cost_estimate=cost(4 * ROWS * WIDE, 5_000_000),
        name="own_and_direct",
    )(ids, sq, own, up2_in, down2_in)

    near = lax.axis_size(("section", "dp"))
    logits, parts = pl.pallas_call(
        total_kernel,
        in_specs=[whole()] * 5,
        out_specs=[whole()] * 2,
        out_shape=(pltpu.VMEM((ROWS, WIDE), F32), shape(near, 8, 128)),
        scratch_shapes=[pltpu.VMEM((ROWS, 1), F32)] * 2,
        compiler_params=vmem(12),
        name="row_totals",
    )(sums, part, target, up3_in, down3_in)
    parts = lax.all_to_all(parts, ("section", "dp"), 0, 0, tiled=True)
    parts = pl.pallas_call(
        join_kernel,
        in_specs=[whole()],
        out_specs=whole(),
        out_shape=shape(lax.axis_size("tp"), 8, 128),
        compiler_params=vmem(2),
        name="join_totals",
    )(parts)
    parts = lax.all_to_all(parts, "tp", 0, 0, tiled=True)
    logprobs, target = pl.pallas_call(
        last_kernel,
        in_specs=[whole(), whole()],
        out_specs=[far(), whole()],
        out_shape=(shape(ROWS, OWN, dtype=BF16), shape(1, ROWS // DP)),
        scratch_shapes=[pltpu.VMEM((ROWS, OWN), BF16), pltpu.VMEM((ROWS, 1), F32), pltpu.SemaphoreType.DMA((6,))],
        compiler_params=vmem(8),
        name="log_probabilities",
    )(logits, parts)
    return logprobs, target.reshape(ROWS // DP)


def solution(mesh):
    placed = (P(None, "dp"), P("dp"), P("dp", ("section", "tp")), P())
    return jax.shard_map(
        body,
        mesh=mesh,
        in_specs=placed,
        out_specs=(P(None, ("section", "tp", "dp")), P("dp")),
        check_vma=False,
    )
```

time: 384 us -> 73.2 us (0.19)
  blocking collectives: 277 us -> 32.5 us
  waiting for transfers between devices: 70.7 us -> 11.4 us
  Pallas kernels: 0 us -> 19 us
  between operations: 14.1 us -> 0.87 us
  matrix products: 11.7 us -> 0 us
  starting transfers between devices: 0.04 us -> 9.22 us
  other arithmetic: 7.08 us -> 0 us
    psum x2 -> x0, blocking collectives: 138 us -> none  [the longest x1 128 us: body(): lax.psum((jnp.sum(jnp.exp(logits - row_top[:, None]), axis=1), picked), (...]
    pmax x1 -> x0, blocking collectives: 125 us -> none  [body(): row_top = lax.pmax(jnp.max(logits, axis=1), ('section', 'tp'))]
    unnamed x2 -> x0, waiting for transfers between devices: 70.7 us -> none
    pallas_call x0 -> x8, Pallas kernels: none -> 19 us  [the longest x1 4.92 us: body(): pl.pallas_call(first_kernel, in_specs=[far(), far(), far()], out_specs=[w...]
    all_to_all x1 -> x2, blocking collectives: 14.8 us -> 32.5 us  [the longest x1 19.1 us: body(): parts = lax.all_to_all(parts, 'tp', 0, 0, tiled=True)]
    dot_general x1 -> x0, matrix products: 11.7 us -> none  [body(): jnp.dot(normed, lm_head, preferred_element_type=jnp.float32)]
    ppermute x0 -> x6, waiting for transfers between devices: none -> 11.4 us  [shifted(): return lax.ppermute(array, 'dp', [(i, (i + k) % DP) for i in range(DP)])]
    ppermute x0 -> x6, starting transfers between devices: none -> 9.22 us  [shifted(): return lax.ppermute(array, 'dp', [(i, (i + k) % DP) for i in range(DP)])]
  transfers between devices with their start and end apart: 1 -> 6, of which waited for: 1 -> 4; matrix products, arithmetic and copies ran while one was open for 0% -> 0% of each run, Pallas kernels for 0% -> 14%
where the time goes in v2:
time: 73.2 us; the launch traced here: 73 us
  blocking collectives  32.5 us (44%)
  Pallas kernels  19 us (26%)
  waiting for transfers between devices  11.4 us (16%)
  starting transfers between devices  9.22 us (13%)
  between operations  0.87 us (1%)
    all_to_all x1, blocking collectives, body(): parts = lax.all_to_all(parts, 'tp', 0, 0, tiled=True)  19.1 us
    all_to_all x1, blocking collectives, body(): parts = lax.all_to_all(parts, ('section', 'dp'), 0, 0, tiled=True)  13.4 us
    ppermute x6, waiting for transfers between devices, shifted(): return lax.ppermute(array, 'dp', [(i, (i + k) % DP) for i in range(DP)])  11.4 us
    ppermute x6, starting transfers between devices, shifted(): return lax.ppermute(array, 'dp', [(i, (i + k) % DP) for i in range(DP)])  9.22 us
    pallas_call x1, Pallas kernels, body(): pl.pallas_call(first_kernel, in_specs=[far(), far(), far()], out_specs=[w...  4.92 us
    pallas_call x1, Pallas kernels, body(): pl.pallas_call(own_kernel, in_specs=[whole(), far()], out_specs=whole(),...  4.03 us
    pallas_call x1, Pallas kernels, body(): pl.pallas_call(passing_kernel, in_specs=[whole()] * 6, out_specs=[whole()...  2.62 us
    pallas_call x1, Pallas kernels, body(): pl.pallas_call(direct_kernel, in_specs=[whole()] * 4, out_specs=[whole()]...  2.61 us
  transfers between devices with their start and end apart: 6, of which 4 were waited for; matrix products, arithmetic and copies ran while one was open for 0% of the time, Pallas kernels for 14%

profile of v2, /device:TPU:1, one launch (start us, length us, event | category | flops | bytes accessed | tf_op | source)
XLA Modules:
  0.0 73.0 jit_solution(6503126525813141503)
XLA Ops:
  0.6 4.9 %first_window.1 = (bf16[672,2048]{1,0:T(8,128)(2,1)S(1)}, f32[672,128]{1,0:T(8,128)S(1)}, bf16[336,640]{1,0:T(8,128)(2,1)S(1)}, bf16[336,640]{1,0:T(8,128)(2,1)S...) custom-call(bf16[672,2048]{1,0:T(8,128)(2,1)} %x_ref.1, f32[1,2048]{1,0:T(1,128)} %bitcast.5, ...), custom_call_target="tpu_custom_call" | custom-call | flops 1761607680 | bytes 10000000 | tf_op jit(solution)/shard_map/first_window/pallas_call | solution.py:247
  5.6 2.2 %collective-permute-start.2 = (bf16[336,640]{1,0:T(8,128)(2,1)S(1)}, bf16[336,640]{1,0:T(8,128)(2,1)S(1)}, u32[]{:S(2)}, u32[]{:S(2)}) collective-permute-start(bf16[336,640]{1,0:T(8,128)(2,1)S(1)} %get-tuple-element.28), channel_id=1, source_target_pairs={{0,1},{1,2},{2,3},{3,0},{4,5},{5,6},{6,7},{7,4},{8,9},{9,10},{10,1... | collective-permute-start | bytes 1290248 | tf_op jit(solution)/shard_map/ppermute | solution.py:264
  7.8 1.5 %collective-permute-start.3 = (bf16[336,640]{1,0:T(8,128)(2,1)S(1)}, bf16[336,640]{1,0:T(8,128)(2,1)S(1)}, u32[]{:S(2)}, u32[]{:S(2)}) collective-permute-start(bf16[336,640]{1,0:T(8,128)(2,1)S(1)} %get-tuple-element.29), channel_id=1, source_target_pairs={{0,3},{1,0},{2,1},{3,2},{4,7},{5,4},{6,5},{7,6},{8,11},{9,8},{10,9... | collective-permute-start | bytes 1290248 | tf_op jit(solution)/shard_map/ppermute | solution.py:264
  9.3 2.6 %direct_windows.1 = (bf16[336,640]{1,0:T(8,128)(2,1)S(1)}, bf16[336,640]{1,0:T(8,128)(2,1)S(1)}) custom-call(bf16[672,2048]{1,0:T(8,128)(2,1)S(1)} %get-tuple-element.20.hg_ref, f32[672,128]{1,0:T(8,128)S(1)} %get-tuple-element.19.sq_ref, bf16[640,2048]{1,0:T(8,128)(2,1)S(1)} %get-tuple-element.21.w_up_ref, bf16[640,2048]{1,0:T(8,128)(2,1)S(1)} %get-tuple-element.22.w_down_ref), custom_call_target="tpu_custom_call" | custom-call | flops 1761607680 | bytes 10000000 | tf_op jit(solution)/shard_map/direct_windows/pallas_call | solution.py:267
  11.9 0.1 collective-permute-start
  12.0 0.0 copy-start
  12.0 2.7 %collective-permute-start.1 = (bf16[336,640]{1,0:T(8,128)(2,1)S(1)}, bf16[336,640]{1,0:T(8,128)(2,1)S(1)}, u32[]{:S(2)}, u32[]{:S(2)}) collective-permute-start(bf16[336,640]{1,0:T(8,128)(2,1)S(1)} %get-tuple-element.24), channel_id=1, source_target_pairs={{0,3},{1,0},{2,1},{3,2},{4,7},{5,4},{6,5},{7,6},{8,11},{9,8},{10,9... | collective-permute-start | bytes 1290248 | tf_op jit(solution)/shard_map/ppermute | solution.py:264
  14.7 2.1 %collective-permute-done.2.up_in_ref = bf16[336,640]{1,0:T(8,128)(2,1)S(1)} collective-permute-done((bf16[336,640]{1,0:T(8,128)(2,1)S(1)}, bf16[336,640]{1,0:T(8,128)(2,1)S(1)}, u32[]{:S(2)}, u32[]{:S(2)}) %collective-permute-start.2) | collective-permute-done | bytes 430112 | tf_op jit(solution)/shard_map/ppermute | solution.py:264
  16.8 1.2 %collective-permute-done.3.down_in_ref = bf16[336,640]{1,0:T(8,128)(2,1)S(1)} collective-permute-done((bf16[336,640]{1,0:T(8,128)(2,1)S(1)}, bf16[336,640]{1,0:T(8,128)(2,1)S(1)}, u32[]{:S(2)}, u32[]{:S(2)}) %collective-permute-start.3) | collective-permute-done | bytes 430112 | tf_op jit(solution)/shard_map/ppermute | solution.py:264
  17.9 2.6 %passing_windows.1 = (bf16[336,640]{1,0:T(8,128)(2,1)S(1)}, bf16[336,640]{1,0:T(8,128)(2,1)S(1)}) custom-call(bf16[672,2048]{1,0:T(8,128)(2,1)S(1)} %get-tuple-element.20.hg_ref, f32[672,128]{1,0:T(8,128)S(1)} %get-tuple-element.19.sq_ref, bf16[640,2048]{1,0:T(8,128)(2,1)S(1)} %get-tuple-element.21.w_up_ref, ...), custom_call_target="tpu_custom_call" | custom-call | flops 1761607680 | bytes 10000000 | tf_op jit(solution)/shard_map/passing_windows/pallas_call | solution.py:277
  20.6 1.6 %collective-permute-start.4 = (bf16[336,640]{1,0:T(8,128)(2,1)S(1)}, bf16[336,640]{1,0:T(8,128)(2,1)S(1)}, u32[]{:S(2)}, u32[]{:S(2)}) collective-permute-start(bf16[336,640]{1,0:T(8,128)(2,1)S(1)} %get-tuple-element.30), channel_id=1, source_target_pairs={{0,1},{1,2},{2,3},{3,0},{4,5},{5,6},{6,7},{7,4},{8,9},{9,10},{10,1... | collective-permute-start | bytes 1290248 | tf_op jit(solution)/shard_map/ppermute | solution.py:264
  22.2 1.1 %collective-permute-start.5 = (bf16[336,640]{1,0:T(8,128)(2,1)S(1)}, bf16[336,640]{1,0:T(8,128)(2,1)S(1)}, u32[]{:S(2)}, u32[]{:S(2)}) collective-permute-start(bf16[336,640]{1,0:T(8,128)(2,1)S(1)} %get-tuple-element.31), channel_id=1, source_target_pairs={{0,3},{1,0},{2,1},{3,2},{4,7},{5,4},{6,5},{7,6},{8,11},{9,8},{10,9... | collective-permute-start | bytes 1290248 | tf_op jit(solution)/shard_map/ppermute | solution.py:264
  23.3 0.0 copy-done
  23.3 4.0 %own_window.1.own_ref = f32[672,640]{1,0:T(8,128)S(1)} custom-call(bf16[672,2048]{1,0:T(8,128)(2,1)S(1)} %get-tuple-element.20.hg_ref, bf16[2376,2048]{1,0:T(8,128)(2,1)} %bitcast.4), custom_call_target="tpu_custom_call" | custom-call | flops 1761607680 | bytes 6000000 | tf_op jit(solution)/shard_map/own_window/pallas_call | solution.py:288
  27.4 0.0 collective-permute-done.up_ref
  27.4 0.0 collective-permute-done.1.down_ref
  27.4 0.9 %own_and_direct.1 = (f32[672,640]{1,0:T(8,128)S(1)}, f32[672,128]{1,0:T(8,128)S(1)}, s32[672,128]{1,0:T(8,128)S(1)}) custom-call(s32[1,672]{1,0:T(1,128)S(1)} %reshape.13.ids_ref, f32[672,128]{1,0:T(8,128)S(1)} %get-tuple-element.19.sq_ref, f32[672,640]{1,0:T(8,128)S(1)} %own_window.1.own_ref, bf16[336,640]{1,0:T(8,128)(2,1)S(1)} %collective-permute-done.up_ref, ...), custom_call_target="tpu_custom_call" | custom-call | flops 1720320 | bytes 5000000 | tf_op jit(solution)/shard_map/own_and_direct/pallas_call | solution.py:298
  28.3 6.9 %collective-permute-done.4.up_ref = bf16[336,640]{1,0:T(8,128)(2,1)S(1)} collective-permute-done((bf16[336,640]{1,0:T(8,128)(2,1)S(1)}, bf16[336,640]{1,0:T(8,128)(2,1)S(1)}, u32[]{:S(2)}, u32[]{:S(2)}) %collective-permute-start.4) | collective-permute-done | bytes 430112 | tf_op jit(solution)/shard_map/ppermute | solution.py:264
  35.2 1.2 %collective-permute-done.5.down_ref = bf16[336,640]{1,0:T(8,128)(2,1)S(1)} collective-permute-done((bf16[336,640]{1,0:T(8,128)(2,1)S(1)}, bf16[336,640]{1,0:T(8,128)(2,1)S(1)}, u32[]{:S(2)}, u32[]{:S(2)}) %collective-permute-start.5) | collective-permute-done | bytes 430112 | tf_op jit(solution)/shard_map/ppermute | solution.py:264
  36.4 2.2 %row_totals.1 = (f32[672,640]{1,0:T(8,128)S(1)}, f32[16,8,128]{2,1,0:T(8,128)S(1)}) custom-call(f32[672,640]{1,0:T(8,128)S(1)} %get-tuple-element.25.sum_ref, f32[672,128]{1,0:T(8,128)S(1)} %get-tuple-element.26.part_ref, s32[672,128]{1,0:T(8,128)S(1)} %get-tuple-element.27.target_ref, bf16[336,640]{1,0:T(8,128)(2,1)S(1)} %collective-permute-done.4.up_ref, ...), custom_call_target="tpu_custom_call" | custom-call | tf_op jit(solution)/shard_map/row_totals/pallas_call | solution.py:309
  38.6 13.4 %all_to_all.10.parts_ref = f32[16,8,128]{2,1,0:T(8,128)S(1)} all-to-all(f32[16,8,128]{2,1,0:T(8,128)S(1)} %get-tuple-element.33), channel_id=1, replica_groups=mesh['section'=4,'tp'=16,'dp'=4] {'section','dp'}, dimensions={0} | all-to-all | bytes 131072 | tf_op jit(solution)/shard_map/all_to_all | solution.py:318
  52.1 19.1 %all_to_all.11.parts_ref = f32[16,8,128]{2,1,0:T(8,128)S(1)} all-to-all(f32[16,8,128]{2,1,0:T(8,128)S(1)} %join_totals.1), channel_id=1, replica_groups=mesh['section'=4,'tp'=16,'dp'=4] {'tp'}, dimensions={0} | all-to-all | bytes 131072 | tf_op jit(solution)/shard_map/all_to_all | solution.py:327
  71.2 1.7 %log_probabilities.1 = (bf16[672,594]{1,0:T(8,128)(2,1)}, f32[1,168]{1,0:T(1,128)}) custom-call(f32[672,640]{1,0:T(8,128)S(1)} %get-tuple-element.32.logits_ref, f32[16,8,128]{2,1,0:T(8,128)S(1)} %all_to_all.11.parts_ref), custom_call_target="tpu_custom_call" | custom-call | tf_op jit(solution)/shard_map/log_probabilities/pallas_call | solution.py:328
  (2 shorter events, 0.0 us)
Async XLA Ops:
  5.6 11.2 %collective-permute-start.2 = (bf16[336,640]{1,0:T(8,128)(2,1)S(1)}, bf16[336,640]{1,0:T(8,128)(2,1)S(1)}, u32[]{:S(2)}, u32[]{:S(2)}) collective-permute-start(bf16[336,640]{1,0:T(8,128)(2,1)S(1)} %get-tuple-element.28), channel_id=1, source_target_pairs={{0,1},{1,2},{2,3},{3,0},{4,5},{5,6},{6,7},{7,4},{8,9},{9,10},{10,1... | collective-permute-start | bytes 1290248 | tf_op jit(solution)/shard_map/ppermute | solution.py:264
  7.8 10.2 %collective-permute-start.3 = (bf16[336,640]{1,0:T(8,128)(2,1)S(1)}, bf16[336,640]{1,0:T(8,128)(2,1)S(1)}, u32[]{:S(2)}, u32[]{:S(2)}) collective-permute-start(bf16[336,640]{1,0:T(8,128)(2,1)S(1)} %get-tuple-element.29), channel_id=1, source_target_pairs={{0,3},{1,0},{2,1},{3,2},{4,7},{5,4},{6,5},{7,6},{8,11},{9,8},{10,9... | collective-permute-start | bytes 1290248 | tf_op jit(solution)/shard_map/ppermute | solution.py:264
  11.9 15.5 %collective-permute-start = (bf16[336,640]{1,0:T(8,128)(2,1)S(1)}, bf16[336,640]{1,0:T(8,128)(2,1)S(1)}, u32[]{:S(2)}, u32[]{:S(2)}) collective-permute-start(bf16[336,640]{1,0:T(8,128)(2,1)S(1)} %get-tuple-element.23), channel_id=1, source_target_pairs={{0,1},{1,2},{2,3},{3,0},{4,5},{5,6},{6,7},{7,4},{8,9},{9,10},{10,1... | collective-permute-start | bytes 1290248 | tf_op jit(solution)/shard_map/ppermute | solution.py:264
  12.0 11.3 %copy-start = (s32[672]{0:T(1024)S(1)}, s32[672]{0:T(1024)}, u32[]{:S(2)}) copy-start(s32[672]{0:T(1024)} %param.7) | copy-start | bytes 8068
  12.0 15.4 %collective-permute-start.1 = (bf16[336,640]{1,0:T(8,128)(2,1)S(1)}, bf16[336,640]{1,0:T(8,128)(2,1)S(1)}, u32[]{:S(2)}, u32[]{:S(2)}) collective-permute-start(bf16[336,640]{1,0:T(8,128)(2,1)S(1)} %get-tuple-element.24), channel_id=1, source_target_pairs={{0,3},{1,0},{2,1},{3,2},{4,7},{5,4},{6,5},{7,6},{8,11},{9,8},{10,9... | collective-permute-start | bytes 1290248 | tf_op jit(solution)/shard_map/ppermute | solution.py:264
  20.6 14.6 %collective-permute-start.4 = (bf16[336,640]{1,0:T(8,128)(2,1)S(1)}, bf16[336,640]{1,0:T(8,128)(2,1)S(1)}, u32[]{:S(2)}, u32[]{:S(2)}) collective-permute-start(bf16[336,640]{1,0:T(8,128)(2,1)S(1)} %get-tuple-element.30), channel_id=1, source_target_pairs={{0,1},{1,2},{2,3},{3,0},{4,5},{5,6},{6,7},{7,4},{8,9},{9,10},{10,1... | collective-permute-start | bytes 1290248 | tf_op jit(solution)/shard_map/ppermute | solution.py:264
  22.2 14.2 %collective-permute-start.5 = (bf16[336,640]{1,0:T(8,128)(2,1)S(1)}, bf16[336,640]{1,0:T(8,128)(2,1)S(1)}, u32[]{:S(2)}, u32[]{:S(2)}) collective-permute-start(bf16[336,640]{1,0:T(8,128)(2,1)S(1)} %get-tuple-element.31), channel_id=1, source_target_pairs={{0,3},{1,0},{2,1},{3,2},{4,7},{5,4},{6,5},{7,6},{8,11},{9,8},{10,9... | collective-permute-start | bytes 1290248 | tf_op jit(solution)/shard_map/ppermute | solution.py:264

commit v3 on v2

v3 whole, which is shorter than its diff:
```python
import jax
import jax.numpy as jnp
from jax import lax
from jax.experimental import pallas as pl
from jax.experimental.pallas import tpu as pltpu
from jax.sharding import PartitionSpec as P

D = 8192
EPSILON = 1e-06
ROWS = 672
HALF = ROWS // 2
QUARTER = ROWS // 4
FREE = QUARTER - 128
EARLY = 240
DP = 4
OWN = 594
STEP = 592
SPAN = 600
WIDE = 640
LAST = 512
OVER = OWN - LAST
PLACE = 3 * OVER - 128
BLOCK = 112
PIECE = 48
F32 = jnp.float32
BF16 = jnp.bfloat16
CONTRACT = (((1,), (1,)), ((), ()))


def whole():
    return pl.BlockSpec(memory_space=pltpu.VMEM)


def far():
    return pl.BlockSpec(memory_space=pltpu.HBM)


def vmem(mib):
    return pltpu.CompilerParams(vmem_limit_bytes=mib * 1024 * 1024)


def shape(*dims, dtype=F32):
    return jax.ShapeDtypeStruct(dims, dtype)


def cost(flops, nbytes):
    return pl.CostEstimate(flops=flops, bytes_accessed=nbytes, transcendentals=0)


def lane_of(dims):
    return lax.broadcasted_iota(jnp.int32, dims, 1)


def row_of(dims):
    return lax.broadcasted_iota(jnp.int32, dims, 0)


def to_lanes(column, begin=0):
    dims = (column.shape[0], 128)
    return jnp.sum(jnp.where(row_of(dims) + begin == lane_of(dims), column, 0.0), axis=0, keepdims=True)


def to_column(row, n=128):
    return jnp.sum(jnp.where(row_of((n, 128)) == lane_of((n, 128)), row, 0.0), axis=1, keepdims=True)


def lane_groups():
    return [(k, begin, min(128, ROWS - begin)) for k, begin in enumerate(range(0, ROWS, 128))]


def window_copy(w_ref, chunk, held_ref, sem):
    rows = pl.ds(pl.multiple_of(lax.rem(chunk, DP) * STEP, 16), SPAN)
    return pltpu.make_async_copy(w_ref.at[rows], held_ref.at[pl.ds(0, SPAN)], sem)


def dot(left, right):
    return lax.dot_general(left, right, CONTRACT, preferred_element_type=F32)


def message(rows):
    return pltpu.VMEM((rows + rows // 6, LAST), BF16)


def pack(out_ref, logits, squares):
    n = logits.shape[0]
    third, sixth = n // 3, n // 6
    out_ref[:n, :] = logits[:, :LAST].astype(BF16)
    over = [logits[k * third : k * third + third, LAST:] for k in range(3)]
    lane = lane_of((third, 128))
    middle = pltpu.roll(over[1], OVER, 1)
    first = jnp.where(lane < OVER, over[0], middle)
    second = jnp.where(lane < 2 * OVER - 128, middle, pltpu.roll(over[2], 2 * OVER - 128, 1))
    for k in range(3):
        total = squares[k * third : k * third + third]
        high = total.astype(BF16).astype(F32)
        mid = (total - high).astype(BF16).astype(F32)
        for place, term in enumerate((high, mid, total - high - mid)):
            second = jnp.where(lane == PLACE + 3 * k + place, term, second)
    second = jnp.where(lane < PLACE + 9, second, 0.0)
    for i in (0, 1):
        for j, tile in enumerate((first, second)):
            begin = 256 * i + 128 * j
            out_ref[n:, begin : begin + 128] = tile[i * sixth : i * sixth + sixth].astype(BF16)


def unpack(in_ref, n):
    third = n // 3
    rest = in_ref[n : n + n // 6, :].astype(F32)
    first = jnp.concatenate([rest[:, 0:128], rest[:, 256:384]], axis=0)
    second = jnp.concatenate([rest[:, 128:256], rest[:, 384:512]], axis=0)
    lane = lane_of((third, 128))
    middle = jnp.where(lane < 128 - OVER, pltpu.roll(first, 128 - OVER, 1), pltpu.roll(second, 128 - OVER, 1))
    over = jnp.concatenate([first, middle, pltpu.roll(second, 2 * (128 - OVER), 1)], axis=0)
    squares = []
    for k in range(3):
        held = (lane >= PLACE + 3 * k) & (lane < PLACE + 3 * k + 3)
        squares.append(jnp.sum(jnp.where(held, second, 0.0), axis=1, keepdims=True))
    return over, jnp.concatenate(squares, axis=0)


def aligned(logits, offset):
    chunk = lax.rem(lax.axis_index("dp") + offset, DP)
    return pltpu.roll(logits, lax.rem(WIDE - (OWN - STEP) * chunk, WIDE), 1)


def scaled(x, g_ref, hg_ref, sq_ref, at):
    for begin in range(at, at + HALF, PIECE):
        rows = slice(begin, begin + PIECE)
        total = jnp.zeros((PIECE, 128), F32)
        for k in range(0, x.shape[1], 128):
            part = x[rows, k : k + 128].astype(F32)
            hg_ref[rows, k : k + 128] = (part * g_ref[:, k : k + 128]).astype(BF16)
            total = total + part * part
        sq_ref[rows, :] = jnp.broadcast_to(jnp.sum(total, axis=1, keepdims=True), (PIECE, 128))


def first_kernel(x_ref, g_ref, w_ref, hg_ref, sq_ref, up_ref, down_ref, x_held, g_held, w_held, sem):
    g_copy = pltpu.make_async_copy(g_ref, g_held, sem.at[0])
    w_copy = window_copy(w_ref, lax.axis_index("dp") + 2, w_held, sem.at[1])
    x_copies = []
    for half in (0, 1):
        rows = pl.ds(half * HALF, HALF)
        x_copies.append(pltpu.make_async_copy(x_ref.at[rows], x_held.at[rows], sem.at[2 + half]))
    for copy in [g_copy, *x_copies, w_copy]:
        copy.start()
    g_copy.wait()
    for half in (0, 1):
        x_copies[half].wait()
        scaled(x_held, g_held, hg_ref, sq_ref, half * HALF)
    w_copy.wait()
    for half, out_ref in ((0, up_ref), (1, down_ref)):
        rows = slice(half * HALF, half * HALF + HALF)
        pack(out_ref, aligned(dot(hg_ref[rows, :], w_held[...]), 2), sq_ref[rows, :])


def direct_kernel(hg_ref, sq_ref, w_ref, up_ref, down_ref, w_up_ref, w_down_ref, sem):
    copies = []
    for i, held_ref in enumerate((w_up_ref, w_down_ref)):
        copies.append(window_copy(w_ref, lax.axis_index("dp") + 1 + 2 * i, held_ref, sem.at[i]))
        copies[-1].start()
    for copy in copies:
        copy.wait()
    for i, (held_ref, out_ref) in enumerate(((w_up_ref, up_ref), (w_down_ref, down_ref))):
        rows = slice(HALF - i * HALF, ROWS - i * HALF)
        pack(out_ref, aligned(dot(hg_ref[rows, :], held_ref[...]), 1 + 2 * i), sq_ref[rows, :])


def passing_kernel(hg_ref, sq_ref, w_up_ref, w_down_ref, up_in_ref, down_in_ref, w_ref, *outs):
    outs, (w_own_ref, sem) = outs[:4], outs[4:]
    copy = window_copy(w_ref, lax.axis_index("dp"), w_own_ref, sem.at[0])
    copy.start()
    for i, (held_ref, in_ref) in enumerate(((w_up_ref, up_in_ref), (w_down_ref, down_in_ref))):
        rows = slice(i * HALF, i * HALF + HALF)
        over, squares = unpack(in_ref, HALF)
        came = jnp.concatenate([in_ref[:HALF, :].astype(F32), over], axis=1)
        total = sq_ref[rows, :] + squares
        logits = aligned(dot(hg_ref[rows, :], held_ref[...]), 1 + 2 * i) + came
        for k, part in ((0, slice(0, EARLY)), (1, slice(EARLY, HALF))):
            pack(outs[2 * k + i], logits[part], total[part])
    copy.wait()


def own_kernel(hg_ref, w_own_ref, own_ref):
    own_ref[...] = dot(hg_ref[...], w_own_ref[...])


def part_kernel(ids_ref, sq_ref, own_ref, up_ref, down_ref, sum_ref, part_ref, target_ref):
    group = lax.axis_index("section") * lax.axis_size("tp") + lax.axis_index("tp")
    base = (group * DP + lax.axis_index("dp")) * OWN
    for k, begin, n in lane_groups():
        same = row_of((n, n)) == lane_of((n, n))
        ids = jnp.sum(jnp.where(same, ids_ref[:, begin : begin + n].astype(F32), 0.0), axis=1, keepdims=True)
        target = ids.astype(jnp.int32) - base
        target_ref[begin : begin + n, :] = jnp.broadcast_to(jnp.where(target < OWN, target, -1), (n, 128))
    for half, came_ref in ((0, down_ref), (1, up_ref)):
        over, squares = unpack(came_ref, HALF)
        part_ref[half * HALF : half * HALF + HALF, :] = sq_ref[half * HALF : half * HALF + HALF, :] + squares
        for begin in range(0, HALF, BLOCK):
            rows, part = slice(half * HALF + begin, half * HALF + begin + BLOCK), slice(begin, begin + BLOCK)
            own = aligned(own_ref[rows, :], 0)
            sum_ref[rows, :LAST] = own[:, :LAST] + came_ref[part, :].astype(F32)
            sum_ref[rows, LAST:] = own[:, LAST:] + over[part]


def block_totals(at, n, sum_ref, part_ref, target_ref, came_ref, logits_ref, to, over_ref, scale_ref, lse_ref, picked_ref):
    over, squares = unpack(came_ref, n)
    over_ref[...] = over
    scale_ref[...] = lax.rsqrt((part_ref[at : at + n, :] + squares) / D + EPSILON)
    for begin in range(0, n, PIECE):
        rows, part, out = (slice(start + begin, start + begin + PIECE) for start in (at, 0, to))
        lane = lane_of((PIECE, 128))
        scale, target = scale_ref[part, :], target_ref[rows, :]
        tiles = []
        for k in range(0, WIDE, 128):
            came = over_ref[part, :] if k == LAST else came_ref[part, k : k + 128].astype(F32)
            tile = (sum_ref[rows, k : k + 128] + came) * scale
            logits_ref[out, k : k + 128] = tile
            tiles.append(jnp.where(lane < OVER, tile, -jnp.inf) if k == LAST else tile)
        top = tiles[0]
        for tile in tiles[1:]:
            top = jnp.maximum(top, tile)
        top = jnp.max(top, axis=1, keepdims=True)
        total = picked = jnp.zeros((PIECE, 128), F32)
        for k, tile in enumerate(tiles):
            total = total + jnp.exp(tile - top)
            picked = picked + jnp.where(lane == target - 128 * k, tile, 0.0)
        lse_ref[part, :] = top + jnp.log(jnp.sum(total, axis=1, keepdims=True))
        picked_ref[part, :] = jnp.sum(picked, axis=1, keepdims=True)


def totals_scratch(n):
    return [pltpu.VMEM((2, n, lanes), F32) for lanes in (128, 128, 1, 1)]


def early_kernel(sum_ref, part_ref, target_ref, up_ref, down_ref, logits_ref, out_ref, *scratch):
    out_ref[...] = jnp.zeros(out_ref.shape, F32)
    for half, came_ref in ((0, up_ref), (1, down_ref)):
        held = [ref.at[half] for ref in scratch]
        block_totals(half * HALF, EARLY, sum_ref, part_ref, target_ref, came_ref, logits_ref, half * EARLY, *held)
        for first, column in zip((4 * half, 8 + 4 * half), held[2:]):
            for k, (begin, end) in enumerate(((0, 128), (128, QUARTER), (QUARTER, EARLY))):
                out_ref[first + k : first + k + 1, :] = to_lanes(column[begin:end, :])


def late_kernel(sum_ref, part_ref, target_ref, up_ref, down_ref, early_ref, logits_ref, out_ref, *scratch):
    late = HALF - EARLY
    row = row_of(early_ref.shape)
    rows = early_ref[...]
    for half, came_ref in ((0, up_ref), (1, down_ref)):
        held = [ref.at[half] for ref in scratch]
        block_totals(half * HALF + EARLY, late, sum_ref, part_ref, target_ref, came_ref, logits_ref, half * late, *held)
        for first, column in zip((4 * half, 8 + 4 * half), held[2:]):
            begun = EARLY - QUARTER
            rows = jnp.where(row == first + 2, rows + to_lanes(column[: 128 - begun, :], begun), rows)
            rows = jnp.where(row == first + 3, to_lanes(column[128 - begun :, :]), rows)
    out_ref[...] = jnp.broadcast_to(rows[None], out_ref.shape)


def join_kernel(parts_ref, out_ref):
    lse = joined(parts_ref[:, :8, :])
    picked = jnp.sum(parts_ref[:, 8:, :], axis=0)
    row, lane = row_of((8, 128)), lane_of((8, 128))
    for k in range(DP):
        first, second = (jnp.broadcast_to(picked[2 * k + i : 2 * k + i + 1, :], (8, 128)) for i in (0, 1))
        both = jnp.where((row == 1) & (lane >= FREE), pltpu.roll(first, FREE, 1), lse)
        both = jnp.where((row == 3) & (lane >= FREE), pltpu.roll(first, 2 * FREE, 1), both)
        both = jnp.where((row == 5) & (lane >= FREE), pltpu.roll(second, FREE, 1), both)
        for part in range(k, out_ref.shape[0], DP):
            out_ref[part, :, :] = both


def joined(parts):
    top = jnp.max(parts, axis=0)
    return top + jnp.log(jnp.sum(jnp.exp(parts - top[None]), axis=0))


def last_kernel(early_ref, late_ref, parts_ref, out_ref, target_ref, out_held, lse_held, column_ref, out_sem):
    parts = parts_ref[...]
    lse = joined(parts)
    lse_held[...] = lse
    copies = []
    for half in (0, 1):
        for k, begin, n in ((0, 0, 128), (1, 128, FREE), (2, QUARTER, 128), (3, QUARTER + 128, FREE)):
            column_ref[half * HALF + begin : half * HALF + begin + n, :] = to_column(lse[4 * half + k : 4 * half + k + 1, :], n)
    for half in (0, 1):
        for begin, n, logits_ref in ((0, EARLY, early_ref), (EARLY, HALF - EARLY, late_ref)):
            for piece in range(0, n, PIECE):
                rows = slice(half * HALF + begin + piece, half * HALF + begin + piece + PIECE)
                logits = logits_ref[half * n + piece : half * n + piece + PIECE, :]
                out_held[rows, :] = (logits - column_ref[rows, :])[:, :OWN].astype(BF16)
            rows = pl.ds(half * HALF + begin, n)
            copies.append(pltpu.make_async_copy(out_held.at[rows], out_ref.at[rows], out_sem.at[len(copies)]))
            copies[-1].start()
    picked = jnp.sum(parts, axis=0)
    lane = lane_of((1, 128))
    first = jnp.where(lane < 128 - FREE, pltpu.roll(picked[1:2, :], 128 - FREE, 1), pltpu.roll(picked[3:4, :], 128 - 2 * FREE, 1))
    second = pltpu.roll(picked[5:6, :], 128 - FREE, 1)
    place = 2 * lax.axis_index("dp")
    target_ref[:, 0:128] = first - lse_held[pl.ds(place, 1), :]
    target_ref[:, 128:QUARTER] = (second - lse_held[pl.ds(place + 1, 1), :])[:, : QUARTER - 128]
    for copy in copies:
        copy.wait()


def body(hidden_states, norm_gain, lm_head, target_ids):
    width = hidden_states.shape[1]
    hidden_states = pltpu.with_memory_space_constraint(hidden_states, pltpu.HBM)
    weights = pltpu.with_memory_space_constraint(lm_head.T, pltpu.HBM)
    gain = pltpu.with_memory_space_constraint(norm_gain.reshape(1, width), pltpu.HBM)
    ids = target_ids.reshape(1, ROWS)
    sent = message(HALF)
    window = pltpu.VMEM((WIDE, width), BF16)
    window_flops = 2 * ROWS * WIDE * width

    hg, sq, up1, down1 = pl.pallas_call(
        first_kernel,
        in_specs=[far(), far(), far()],
        out_specs=[whole()] * 4,
        out_shape=(pltpu.VMEM((ROWS, width), BF16), pltpu.VMEM((ROWS, 128), F32), sent, sent),
        scratch_shapes=[
            pltpu.VMEM((ROWS, width), BF16),
            pltpu.VMEM((1, width), F32),
            window,
            pltpu.SemaphoreType.DMA((4,)),
        ],
        compiler_params=vmem(12),
        cost_estimate=cost(window_flops, 10_000_000),
        name="first_window",
    )(hidden_states, gain, weights)

    def shifted(array, k):
        return lax.ppermute(array, "dp", [(i, (i + k) % DP) for i in range(DP)])

    up1_in, down1_in = shifted(up1, 1), shifted(down1, -1)
    up2, down2, w_up, w_down = pl.pallas_call(
        direct_kernel,
        in_specs=[whole()] * 2 + [far()],
        out_specs=[whole()] * 4,
        out_shape=(sent, sent, window, window),
        scratch_shapes=[pltpu.SemaphoreType.DMA((2,))],
        compiler_params=vmem(8),
        cost_estimate=cost(window_flops, 10_000_000),
        name="direct_windows",
    )(hg, sq, weights)
    up2_in, down2_in = shifted(up2, 1), shifted(down2, -1)
    *passing, w_own = pl.pallas_call(
        passing_kernel,
        in_specs=[whole()] * 6 + [far()],
        out_specs=[whole()] * 5,
        out_shape=(message(EARLY),) * 2 + (message(HALF - EARLY),) * 2 + (window,),
        scratch_shapes=[pltpu.SemaphoreType.DMA((1,))],
        compiler_params=vmem(8),
        cost_estimate=cost(window_flops, 10_000_000),
        name="passing_windows",
    )(hg, sq, w_up, w_down, up1_in, down1_in, weights)
    up3a, down3a, up3b, down3b = (shifted(array, k) for array, k in zip(passing, (1, -1, 1, -1)))

    own = pl.pallas_call(
        own_kernel,
        in_specs=[whole()] * 2,
        out_specs=whole(),
        out_shape=pltpu.VMEM((ROWS, WIDE), F32),
        compiler_params=vmem(8),
        cost_estimate=cost(window_flops, 6_000_000),
        name="own_window",
    )(hg, w_own)
    sums, part, target = pl.pallas_call(
        part_kernel,
        in_specs=[whole()] * 5,
        out_specs=[whole()] * 3,
        out_shape=(pltpu.VMEM((ROWS, WIDE), F32), pltpu.VMEM((ROWS, 128), F32), pltpu.VMEM((ROWS, 128), jnp.int32)),
        compiler_params=vmem(10),
        cost_estimate=cost(4 * ROWS * WIDE, 5_000_000),
        name="own_and_direct",
    )(ids, sq, own, up2_in, down2_in)

    early, early_rows = pl.pallas_call(
        early_kernel,
        in_specs=[whole()] * 5,
        out_specs=[whole()] * 2,
        out_shape=(pltpu.VMEM((2 * EARLY, WIDE), F32), shape(16, 128)),
        scratch_shapes=totals_scratch(EARLY),
        compiler_params=vmem(8),
        name="early_totals",
    )(sums, part, target, up3a, down3a)
    late, parts = pl.pallas_call(
        late_kernel,
        in_specs=[whole()] * 6,
        out_specs=[whole()] * 2,
        out_shape=(pltpu.VMEM((ROWS - 2 * EARLY, WIDE), F32), shape(lax.axis_size("tp"), 16, 128)),
        scratch_shapes=totals_scratch(HALF - EARLY),
        compiler_params=vmem(8),
        name="late_totals",
    )(sums, part, target, up3b, down3b, early_rows)
    parts = lax.all_to_all(parts, "tp", 0, 0, tiled=True)
    parts = pl.pallas_call(
        join_kernel,
        in_specs=[whole()],
        out_specs=whole(),
        out_shape=shape(lax.axis_size(("section", "dp")), 8, 128),
        compiler_params=vmem(2),
        name="join_totals",
    )(parts)
    parts = lax.all_to_all(parts, ("section", "dp"), 0, 0, tiled=True)
    logprobs, target = pl.pallas_call(
        last_kernel,
        in_specs=[whole()] * 3,
        out_specs=[far(), whole()],
        out_shape=(shape(ROWS, OWN, dtype=BF16), shape(1, ROWS // DP)),
        scratch_shapes=[pltpu.VMEM((ROWS, OWN), BF16), pltpu.VMEM((8, 128), F32), pltpu.VMEM((ROWS, 1), F32), pltpu.SemaphoreType.DMA((DP,))],
        compiler_params=vmem(8),
        name="log_probabilities",
    )(early, late, parts)
    return logprobs, target.reshape(ROWS // DP)


def solution(mesh):
    placed = (P(None, "dp"), P("dp"), P("dp", ("section", "tp")), P())
    return jax.shard_map(
        body,
        mesh=mesh,
        in_specs=placed,
        out_specs=(P(None, ("section", "tp", "dp")), P("dp")),
        check_vma=False,
    )
```

time: 73.2 us -> 70.4 us (0.962)
  waiting for transfers between devices: 11.4 us -> 2.99 us
  starting transfers between devices: 9.22 us -> 12.6 us
  Pallas kernels: 19 us -> 21 us
    ppermute x6 -> x8, waiting for transfers between devices: 11.4 us -> 2.99 us  [shifted(): return lax.ppermute(array, 'dp', [(i, (i + k) % DP) for i in range(DP)])]
    ppermute x6 -> x8, starting transfers between devices: 9.22 us -> 12.6 us  [shifted(): return lax.ppermute(array, 'dp', [(i, (i + k) % DP) for i in range(DP)])]
    pallas_call x5 -> x6, Pallas kernels: 13.1 us -> 14.7 us  [the longest x1 5.08 us: body(): pl.pallas_call(direct_kernel, in_specs=[whole()] * 2 + [far()], out_specs...]
  transfers between devices with their start and end apart: 6 -> 8, of which waited for: 4 -> 5; matrix products, arithmetic and copies ran while one was open for 0% -> 0% of each run, Pallas kernels for 14% -> 19%
where the time goes in v3:
time: 70.4 us; the launch traced here: 70.2 us
  blocking collectives  32.7 us (46%)
  Pallas kernels  21 us (30%)
  starting transfers between devices  12.6 us (18%)
  waiting for transfers between devices  2.99 us (4%)
  between operations  0.87 us (1%)
    all_to_all x1, blocking collectives, body(): parts = lax.all_to_all(parts, 'tp', 0, 0, tiled=True)  19.8 us
    all_to_all x1, blocking collectives, body(): parts = lax.all_to_all(parts, ('section', 'dp'), 0, 0, tiled=True)  12.9 us
    ppermute x8, starting transfers between devices, shifted(): return lax.ppermute(array, 'dp', [(i, (i + k) % DP) for i in range(DP)])  12.6 us
    pallas_call x1, Pallas kernels, body(): pl.pallas_call(first_kernel, in_specs=[far(), far(), far()], out_specs=[w...  5.23 us
    pallas_call x1, Pallas kernels, body(): pl.pallas_call(direct_kernel, in_specs=[whole()] * 2 + [far()], out_specs...  5.08 us
    pallas_call x1, Pallas kernels, body(): pl.pallas_call(passing_kernel, in_specs=[whole()] * 6 + [far()], out_spec...  3.54 us
    ppermute x8, waiting for transfers between devices, shifted(): return lax.ppermute(array, 'dp', [(i, (i + k) % DP) for i in range(DP)])  2.99 us
    pallas_call x1, Pallas kernels, body(): pl.pallas_call(own_kernel, in_specs=[whole()] * 2, out_specs=whole(), out...  2.33 us
  transfers between devices with their start and end apart: 8, of which 5 were waited for; matrix products, arithmetic and copies ran while one was open for 0% of the time, Pallas kernels for 19%

profile of v3, /device:TPU:1, one launch (start us, length us, event | category | flops | bytes accessed | tf_op | source)
XLA Modules:
  0.0 70.2 jit_solution(4441942835373658952)
XLA Ops:
  0.6 5.2 %first_window.1 = (bf16[672,2048]{1,0:T(8,128)(2,1)S(1)}, f32[672,128]{1,0:T(8,128)S(1)}, bf16[392,512]{1,0:T(8,128)(2,1)S(1)}, bf16[392,512]{1,0:T(8,128)(2,1)S(1)}) custom-call(bf16[672,2048]{1,0:T(8,128)(2,1)} %x_ref.1, f32[1,2048]{1,0:T(1,128)} %bitcast.6, bf16[2376,2048]{1,0:T(8,128)(2,1)} %bitcast.3), custom_call_target="tpu_custom_call" | custom-call | flops 1761607680 | bytes 10000000 | tf_op jit(solution)/shard_map/first_window/pallas_call | solution.py:315
  5.9 2.2 %collective-permute-start = (bf16[392,512]{1,0:T(8,128)(2,1)S(1)}, bf16[392,512]{1,0:T(8,128)(2,1)S(1)}, u32[]{:S(2)}, u32[]{:S(2)}) collective-permute-start(bf16[392,512]{1,0:T(8,128)(2,1)S(1)} %get-tuple-element.28), channel_id=1, source_target_pairs={{0,1},{1,2},{2,3},{3,0},{4,5},{5,6},{6,7},{7,4},{8,9},{9,10},{10,1... | collective-permute-start | bytes 1204232 | tf_op jit(solution)/shard_map/ppermute | solution.py:332
  8.1 1.5 %collective-permute-start.1 = (bf16[392,512]{1,0:T(8,128)(2,1)S(1)}, bf16[392,512]{1,0:T(8,128)(2,1)S(1)}, u32[]{:S(2)}, u32[]{:S(2)}) collective-permute-start(bf16[392,512]{1,0:T(8,128)(2,1)S(1)} %get-tuple-element.29), channel_id=1, source_target_pairs={{0,3},{1,0},{2,1},{3,2},{4,7},{5,4},{6,5},{7,6},{8,11},{9,8},{10,9... | collective-permute-start | bytes 1204232 | tf_op jit(solution)/shard_map/ppermute | solution.py:332
  9.6 5.1 %direct_windows.1 = (bf16[392,512]{1,0:T(8,128)(2,1)S(1)}, bf16[392,512]{1,0:T(8,128)(2,1)S(1)}, bf16[640,2048]{1,0:T(8,128)(2,1)S(1)}, bf16[640,2048]{1,0:T(8,128)(2,1)S(1)}) custom-call(bf16[672,2048]{1,0:T(8,128)(2,1)S(1)} %get-tuple-element.25.hg_ref, f32[672,128]{1,0:T(8,128)S(1)} %get-tuple-element.24.sq_ref, bf16[2376,2048]{1,0:T(8,128)(2,1)} %bitcast.4), custom_call_target="tpu_custom_call" | custom-call | flops 1761607680 | bytes 10000000 | tf_op jit(solution)/shard_map/direct_windows/pallas_call | solution.py:335
  14.7 0.1 collective-permute-start.2
  14.8 2.7 %collective-permute-start.3 = (bf16[392,512]{1,0:T(8,128)(2,1)S(1)}, bf16[392,512]{1,0:T(8,128)(2,1)S(1)}, u32[]{:S(2)}, u32[]{:S(2)}) collective-permute-start(bf16[392,512]{1,0:T(8,128)(2,1)S(1)} %get-tuple-element.32), channel_id=1, source_target_pairs={{0,3},{1,0},{2,1},{3,2},{4,7},{5,4},{6,5},{7,6},{8,11},{9,8},{10,9... | collective-permute-start | bytes 1204232 | tf_op jit(solution)/shard_map/ppermute | solution.py:332
  17.4 0.0 collective-permute-done.up_in_ref
  17.4 0.2 collective-permute-done.1.down_in_ref
  17.6 0.0 copy-start
  17.6 3.5 %passing_windows.1 = (bf16[280,512]{1,0:T(8,128)(2,1)S(1)}, bf16[280,512]{1,0:T(8,128)(2,1)S(1)}, bf16[112,512]{1,0:T(8,128)(2,1)S(1)}, bf16[112,512]{1,0:T(8,128)(2,1)S(1)}, bf16[640,2048]{1,0:T(8,128)(2,1)S(1)}) custom-call(bf16[672,2048]{1,0:T(8,128)(2,1)S(1)} %get-tuple-element.25.hg_ref, f32[672,128]{1,0:T(8,128)S(1)} %get-tuple-element.24.sq_ref, ...), custom_call_target="tpu_custom_call" | custom-call | flops 1761607680 | bytes 10000000 | tf_op jit(solution)/shard_map/passing_windows/pallas_call | solution.py:346
  21.2 1.6 %collective-permute-start.4 = (bf16[280,512]{1,0:T(8,128)(2,1)S(1)}, bf16[280,512]{1,0:T(8,128)(2,1)S(1)}, u32[]{:S(2)}, u32[]{:S(2)}) collective-permute-start(bf16[280,512]{1,0:T(8,128)(2,1)S(1)} %get-tuple-element.36), channel_id=1, source_target_pairs={{0,1},{1,2},{2,3},{3,0},{4,5},{5,6},{6,7},{7,4},{8,9},{9,10},{10,1... | collective-permute-start | bytes 860168 | tf_op jit(solution)/shard_map/ppermute | solution.py:332
  22.8 1.1 %collective-permute-start.5 = (bf16[280,512]{1,0:T(8,128)(2,1)S(1)}, bf16[280,512]{1,0:T(8,128)(2,1)S(1)}, u32[]{:S(2)}, u32[]{:S(2)}) collective-permute-start(bf16[280,512]{1,0:T(8,128)(2,1)S(1)} %get-tuple-element.37), channel_id=1, source_target_pairs={{0,3},{1,0},{2,1},{3,2},{4,7},{5,4},{6,5},{7,6},{8,11},{9,8},{10,9... | collective-permute-start | bytes 860168 | tf_op jit(solution)/shard_map/ppermute | solution.py:332
  23.9 0.0 copy-done
  23.9 0.4 collective-permute-start.6
  24.3 1.0 %collective-permute-done.2.up_ref = bf16[392,512]{1,0:T(8,128)(2,1)S(1)} collective-permute-done((bf16[392,512]{1,0:T(8,128)(2,1)S(1)}, bf16[392,512]{1,0:T(8,128)(2,1)S(1)}, u32[]{:S(2)}, u32[]{:S(2)}) %collective-permute-start.2) | collective-permute-done | bytes 401440 | tf_op jit(solution)/shard_map/ppermute | solution.py:332
  25.3 3.0 %collective-permute-start.7 = (bf16[112,512]{1,0:T(8,128)(2,1)S(1)}, bf16[112,512]{1,0:T(8,128)(2,1)S(1)}, u32[]{:S(2)}, u32[]{:S(2)}) collective-permute-start(bf16[112,512]{1,0:T(8,128)(2,1)S(1)} %get-tuple-element.40), channel_id=1, source_target_pairs={{0,3},{1,0},{2,1},{3,2},{4,7},{5,4},{6,5},{7,6},{8,11},{9,8},{10,9... | collective-permute-start | bytes 344072 | tf_op jit(solution)/shard_map/ppermute | solution.py:332
  28.3 2.3 %own_window.1.own_ref = f32[672,640]{1,0:T(8,128)S(1)} custom-call(bf16[672,2048]{1,0:T(8,128)(2,1)S(1)} %get-tuple-element.25.hg_ref, bf16[640,2048]{1,0:T(8,128)(2,1)S(1)} %get-tuple-element.30.w_own_ref), custom_call_target="tpu_custom_call" | custom-call | flops 1761607680 | bytes 6000000 | tf_op jit(solution)/shard_map/own_window/pallas_call | solution.py:358
  30.6 0.0 collective-permute-done.3.down_ref
  30.6 1.0 %own_and_direct.1 = (f32[672,640]{1,0:T(8,128)S(1)}, f32[672,128]{1,0:T(8,128)S(1)}, s32[672,128]{1,0:T(8,128)S(1)}) custom-call(s32[1,672]{1,0:T(1,128)S(1)} %reshape.13.ids_ref, f32[672,128]{1,0:T(8,128)S(1)} %get-tuple-element.24.sq_ref, f32[672,640]{1,0:T(8,128)S(1)} %own_window.1.own_ref, bf16[392,512]{1,0:T(8,128)(2,1)S(1)} %collective-permute-done.2.up_ref, ...), custom_call_target="tpu_custom_call" | custom-call | flops 1720320 | bytes 5000000 | tf_op jit(solution)/shard_map/own_and_direct/pallas_call | solution.py:367
  31.6 0.0 collective-permute-done.4.up_ref
  31.6 0.8 %collective-permute-done.5.down_ref = bf16[280,512]{1,0:T(8,128)(2,1)S(1)} collective-permute-done((bf16[280,512]{1,0:T(8,128)(2,1)S(1)}, bf16[280,512]{1,0:T(8,128)(2,1)S(1)}, u32[]{:S(2)}, u32[]{:S(2)}) %collective-permute-start.5) | collective-permute-done | bytes 286752 | tf_op jit(solution)/shard_map/ppermute | solution.py:332
  32.4 1.4 %early_totals.1 = (f32[480,640]{1,0:T(8,128)S(1)}, f32[16,128]{1,0:T(8,128)S(1)}) custom-call(f32[672,640]{1,0:T(8,128)S(1)} %get-tuple-element.33.sum_ref, f32[672,128]{1,0:T(8,128)S(1)} %get-tuple-element.34.part_ref, s32[672,128]{1,0:T(8,128)S(1)} %get-tuple-element.35.target_ref, bf16[280,512]{1,0:T(8,128)(2,1)S(1)} %collective-permute-done.4.up_ref, ...), custom_call_target="tpu_custom_call" | custom-call | tf_op jit(solution)/shard_map/early_totals/pallas_call | solution.py:377
  33.8 0.1 collective-permute-done.6.up_ref
  33.9 1.0 %collective-permute-done.7.down_ref = bf16[112,512]{1,0:T(8,128)(2,1)S(1)} collective-permute-done((bf16[112,512]{1,0:T(8,128)(2,1)S(1)}, bf16[112,512]{1,0:T(8,128)(2,1)S(1)}, u32[]{:S(2)}, u32[]{:S(2)}) %collective-permute-start.7) | collective-permute-done | bytes 114720 | tf_op jit(solution)/shard_map/ppermute | solution.py:332
  34.8 0.6 late_totals.1
  35.4 19.8 %all_to_all.10.parts_ref = f32[16,16,128]{2,1,0:T(8,128)S(1)} all-to-all(f32[16,16,128]{2,1,0:T(8,128)S(1)} %get-tuple-element.43), channel_id=1, replica_groups=mesh['section'=4,'tp'=16,'dp'=4] {'tp'}, dimensions={0} | all-to-all | bytes 262144 | tf_op jit(solution)/shard_map/all_to_all | solution.py:395
  55.2 0.1 join_totals.1
  55.3 12.9 %all_to_all.11.parts_ref = f32[16,8,128]{2,1,0:T(8,128)S(1)} all-to-all(f32[16,8,128]{2,1,0:T(8,128)S(1)} %join_totals.1), channel_id=1, replica_groups=mesh['section'=4,'tp'=16,'dp'=4] {'section','dp'}, dimensions={0} | all-to-all | bytes 131072 | tf_op jit(solution)/shard_map/all_to_all | solution.py:404
  68.2 1.8 %log_probabilities.1 = (bf16[672,594]{1,0:T(8,128)(2,1)}, f32[1,168]{1,0:T(1,128)}) custom-call(f32[480,640]{1,0:T(8,128)S(1)} %get-tuple-element.38.early_ref, f32[192,640]{1,0:T(8,128)S(1)} %get-tuple-element.42.late_ref, f32[16,8,128]{2,1,0:T(8,128)S(1)} %all_to_all.11.parts_ref), custom_call_target="tpu_custom_call" | custom-call | tf_op jit(solution)/shard_map/log_probabilities/pallas_call | solution.py:405
  (1 shorter events, 0.0 us)
Async XLA Ops:
  5.9 11.6 %collective-permute-start = (bf16[392,512]{1,0:T(8,128)(2,1)S(1)}, bf16[392,512]{1,0:T(8,128)(2,1)S(1)}, u32[]{:S(2)}, u32[]{:S(2)}) collective-permute-start(bf16[392,512]{1,0:T(8,128)(2,1)S(1)} %get-tuple-element.28), channel_id=1, source_target_pairs={{0,1},{1,2},{2,3},{3,0},{4,5},{5,6},{6,7},{7,4},{8,9},{9,10},{10,1... | collective-permute-start | bytes 1204232 | tf_op jit(solution)/shard_map/ppermute | solution.py:332
  8.1 9.6 %collective-permute-start.1 = (bf16[392,512]{1,0:T(8,128)(2,1)S(1)}, bf16[392,512]{1,0:T(8,128)(2,1)S(1)}, u32[]{:S(2)}, u32[]{:S(2)}) collective-permute-start(bf16[392,512]{1,0:T(8,128)(2,1)S(1)} %get-tuple-element.29), channel_id=1, source_target_pairs={{0,3},{1,0},{2,1},{3,2},{4,7},{5,4},{6,5},{7,6},{8,11},{9,8},{10,9... | collective-permute-start | bytes 1204232 | tf_op jit(solution)/shard_map/ppermute | solution.py:332
  14.7 10.6 %collective-permute-start.2 = (bf16[392,512]{1,0:T(8,128)(2,1)S(1)}, bf16[392,512]{1,0:T(8,128)(2,1)S(1)}, u32[]{:S(2)}, u32[]{:S(2)}) collective-permute-start(bf16[392,512]{1,0:T(8,128)(2,1)S(1)} %get-tuple-element.31), channel_id=1, source_target_pairs={{0,1},{1,2},{2,3},{3,0},{4,5},{5,6},{6,7},{7,4},{8,9},{9,10},{10,1... | collective-permute-start | bytes 1204232 | tf_op jit(solution)/shard_map/ppermute | solution.py:332
  14.8 15.8 %collective-permute-start.3 = (bf16[392,512]{1,0:T(8,128)(2,1)S(1)}, bf16[392,512]{1,0:T(8,128)(2,1)S(1)}, u32[]{:S(2)}, u32[]{:S(2)}) collective-permute-start(bf16[392,512]{1,0:T(8,128)(2,1)S(1)} %get-tuple-element.32), channel_id=1, source_target_pairs={{0,3},{1,0},{2,1},{3,2},{4,7},{5,4},{6,5},{7,6},{8,11},{9,8},{10,9... | collective-permute-start | bytes 1204232 | tf_op jit(solution)/shard_map/ppermute | solution.py:332
  17.6 6.3 %copy-start = (s32[672]{0:T(1024)S(1)}, s32[672]{0:T(1024)}, u32[]{:S(2)}) copy-start(s32[672]{0:T(1024)} %param.7) | copy-start | bytes 8068
  21.2 10.4 %collective-permute-start.4 = (bf16[280,512]{1,0:T(8,128)(2,1)S(1)}, bf16[280,512]{1,0:T(8,128)(2,1)S(1)}, u32[]{:S(2)}, u32[]{:S(2)}) collective-permute-start(bf16[280,512]{1,0:T(8,128)(2,1)S(1)} %get-tuple-element.36), channel_id=1, source_target_pairs={{0,1},{1,2},{2,3},{3,0},{4,5},{5,6},{6,7},{7,4},{8,9},{9,10},{10,1... | collective-permute-start | bytes 860168 | tf_op jit(solution)/shard_map/ppermute | solution.py:332
  22.8 9.5 %collective-permute-start.5 = (bf16[280,512]{1,0:T(8,128)(2,1)S(1)}, bf16[280,512]{1,0:T(8,128)(2,1)S(1)}, u32[]{:S(2)}, u32[]{:S(2)}) collective-permute-start(bf16[280,512]{1,0:T(8,128)(2,1)S(1)} %get-tuple-element.37), channel_id=1, source_target_pairs={{0,3},{1,0},{2,1},{3,2},{4,7},{5,4},{6,5},{7,6},{8,11},{9,8},{10,9... | collective-permute-start | bytes 860168 | tf_op jit(solution)/shard_map/ppermute | solution.py:332
  23.9 9.9 %collective-permute-start.6 = (bf16[112,512]{1,0:T(8,128)(2,1)S(1)}, bf16[112,512]{1,0:T(8,128)(2,1)S(1)}, u32[]{:S(2)}, u32[]{:S(2)}) collective-permute-start(bf16[112,512]{1,0:T(8,128)(2,1)S(1)} %get-tuple-element.39), channel_id=1, source_target_pairs={{0,1},{1,2},{2,3},{3,0},{4,5},{5,6},{6,7},{7,4},{8,9},{9,10},{10,1... | collective-permute-start | bytes 344072 | tf_op jit(solution)/shard_map/ppermute | solution.py:332
  25.3 9.6 %collective-permute-start.7 = (bf16[112,512]{1,0:T(8,128)(2,1)S(1)}, bf16[112,512]{1,0:T(8,128)(2,1)S(1)}, u32[]{:S(2)}, u32[]{:S(2)}) collective-permute-start(bf16[112,512]{1,0:T(8,128)(2,1)S(1)} %get-tuple-element.40), channel_id=1, source_target_pairs={{0,3},{1,0},{2,1},{3,2},{4,7},{5,4},{6,5},{7,6},{8,11},{9,8},{10,9... | collective-permute-start | bytes 344072 | tf_op jit(solution)/shard_map/ppermute | solution.py:332

commit v4 on v3

--- a/solution.py
+++ b/solution.py
@@ -119,8 +119,11 @@
 
 
 def aligned(logits, offset):
-    chunk = lax.rem(lax.axis_index("dp") + offset, DP)
-    return pltpu.roll(logits, lax.rem(WIDE - (OWN - STEP) * chunk, WIDE), 1)
+    shift = (OWN - STEP) * lax.rem(lax.axis_index("dp") + offset, DP)
+    moved = [pltpu.roll(logits[:, k : k + 128], lax.rem(128 - shift, 128), 1) for k in range(0, WIDE, 128)]
+    stays = lane_of(moved[0].shape) < 128 - shift
+    whole_tiles = [jnp.where(stays, tile, after) for tile, after in zip(moved, moved[1:])]
+    return jnp.concatenate(whole_tiles + moved[-1:], axis=1)
 
 
 def scaled(x, g_ref, hg_ref, sq_ref, at):
@@ -274,23 +277,27 @@
     return top + jnp.log(jnp.sum(jnp.exp(parts - top[None]), axis=0))
 
 
-def last_kernel(early_ref, late_ref, parts_ref, out_ref, target_ref, out_held, lse_held, column_ref, out_sem):
+def last_kernel(early_ref, late_ref, parts_ref, out_ref, target_ref, out_held, lse_held, out_sem):
     parts = parts_ref[...]
     lse = joined(parts)
     lse_held[...] = lse
     copies = []
+    pieces = [(begin, 32, 0, begin) for begin in range(0, 128, 32)]
+    pieces += [(128, FREE, 1, 0), (QUARTER, 40, 2, 0), (QUARTER + 40, 32, 2, 40)]
+    pieces += [(EARLY, 32, 2, 72), (EARLY + 32, 24, 2, 104), (QUARTER + 128, FREE, 3, 0)]
     for half in (0, 1):
-        for k, begin, n in ((0, 0, 128), (1, 128, FREE), (2, QUARTER, 128), (3, QUARTER + 128, FREE)):
-            column_ref[half * HALF + begin : half * HALF + begin + n, :] = to_column(lse[4 * half + k : 4 * half + k + 1, :], n)
-    for half in (0, 1):
-        for begin, n, logits_ref in ((0, EARLY, early_ref), (EARLY, HALF - EARLY, late_ref)):
-            for piece in range(0, n, PIECE):
-                rows = slice(half * HALF + begin + piece, half * HALF + begin + piece + PIECE)
-                logits = logits_ref[half * n + piece : half * n + piece + PIECE, :]
-                out_held[rows, :] = (logits - column_ref[rows, :])[:, :OWN].astype(BF16)
-            rows = pl.ds(half * HALF + begin, n)
-            copies.append(pltpu.make_async_copy(out_held.at[rows], out_ref.at[rows], out_sem.at[len(copies)]))
-            copies[-1].start()
+        for begin, n, row, lane in pieces:
+            same = row_of((n, 128)) + lane == lane_of((n, 128))
+            column = jnp.sum(jnp.where(same, lse[4 * half + row : 4 * half + row + 1, :], 0.0), axis=1, keepdims=True)
+            held, size, at = (early_ref, EARLY, begin) if begin < EARLY else (late_ref, HALF - EARLY, begin - EARLY)
+            logits = held[half * size + at : half * size + at + n, :]
+            out = half * HALF + begin
+            out_held[out : out + n, :] = (logits - column)[:, :OWN].astype(BF16)
+            if begin + n in (EARLY, HALF):
+                first = half * HALF + (0 if begin < EARLY else EARLY)
+                rows = pl.ds(first, out + n - first)
+                copies.append(pltpu.make_async_copy(out_held.at[rows], out_ref.at[rows], out_sem.at[len(copies)]))
+                copies[-1].start()
     picked = jnp.sum(parts, axis=0)
     lane = lane_of((1, 128))
     first = jnp.where(lane < 128 - FREE, pltpu.roll(picked[1:2, :], 128 - FREE, 1), pltpu.roll(picked[3:4, :], 128 - 2 * FREE, 1))
@@ -407,7 +414,7 @@
         in_specs=[whole()] * 3,
         out_specs=[far(), whole()],
         out_shape=(shape(ROWS, OWN, dtype=BF16), shape(1, ROWS // DP)),
-        scratch_shapes=[pltpu.VMEM((ROWS, OWN), BF16), pltpu.VMEM((8, 128), F32), pltpu.VMEM((ROWS, 1), F32), pltpu.SemaphoreType.DMA((DP,))],
+        scratch_shapes=[pltpu.VMEM((ROWS, OWN), BF16), pltpu.VMEM((8, 128), F32), pltpu.SemaphoreType.DMA((DP,))],
         compiler_params=vmem(8),
         name="log_probabilities",
     )(early, late, parts)

time: 70.4 us -> 70.1 us (level)
  waiting for transfers between devices: 2.99 us -> 2.09 us
    ppermute x8, waiting for transfers between devices: 2.99 us -> 2.09 us  [shifted(): return lax.ppermute(array, 'dp', [(i, (i + k) % DP) for i in range(DP)])]
  transfers between devices with their start and end apart: 8 -> 8, of which waited for: 5 -> 4; matrix products, arithmetic and copies ran while one was open for 0% -> 0% of each run, Pallas kernels for 19% -> 20%
where the time goes in v4:
time: 70.1 us; the launch traced here: 69.9 us
  blocking collectives  33.2 us (47%)
  Pallas kernels  21.2 us (30%)
  starting transfers between devices  12.5 us (18%)
  waiting for transfers between devices  2.09 us (3%)
  between operations  0.87 us (1%)
    all_to_all x1, blocking collectives, body(): parts = lax.all_to_all(parts, 'tp', 0, 0, tiled=True)  20.3 us
    all_to_all x1, blocking collectives, body(): parts = lax.all_to_all(parts, ('section', 'dp'), 0, 0, tiled=True)  12.9 us
    ppermute x8, starting transfers between devices, shifted(): return lax.ppermute(array, 'dp', [(i, (i + k) % DP) for i in range(DP)])  12.5 us
    pallas_call x1, Pallas kernels, body(): pl.pallas_call(first_kernel, in_specs=[far(), far(), far()], out_specs=[w...  5.12 us
    pallas_call x1, Pallas kernels, body(): pl.pallas_call(direct_kernel, in_specs=[whole()] * 2 + [far()], out_specs...  4.99 us
    pallas_call x1, Pallas kernels, body(): pl.pallas_call(passing_kernel, in_specs=[whole()] * 6 + [far()], out_spec...  4.2 us
    pallas_call x1, Pallas kernels, body(): pl.pallas_call(own_kernel, in_specs=[whole()] * 2, out_specs=whole(), out...  2.33 us
    ppermute x8, waiting for transfers between devices, shifted(): return lax.ppermute(array, 'dp', [(i, (i + k) % DP) for i in range(DP)])  2.09 us
  transfers between devices with their start and end apart: 8, of which 4 were waited for; matrix products, arithmetic and copies ran while one was open for 0% of the time, Pallas kernels for 20%

profile of v4, /device:TPU:1, one launch (start us, length us, event | category | flops | bytes accessed | tf_op | source)
XLA Modules:
  0.0 69.9 jit_solution(7907139436094344395)
XLA Ops:
  0.6 5.1 %first_window.1 = (bf16[672,2048]{1,0:T(8,128)(2,1)S(1)}, f32[672,128]{1,0:T(8,128)S(1)}, bf16[392,512]{1,0:T(8,128)(2,1)S(1)}, bf16[392,512]{1,0:T(8,128)(2,1)S(1)}) custom-call(bf16[672,2048]{1,0:T(8,128)(2,1)} %x_ref.1, f32[1,2048]{1,0:T(1,128)} %bitcast.6, bf16[2376,2048]{1,0:T(8,128)(2,1)} %bitcast.3), custom_call_target="tpu_custom_call" | custom-call | flops 1761607680 | bytes 10000000 | tf_op jit(solution)/shard_map/first_window/pallas_call | solution.py:322
  5.8 2.2 %collective-permute-start = (bf16[392,512]{1,0:T(8,128)(2,1)S(1)}, bf16[392,512]{1,0:T(8,128)(2,1)S(1)}, u32[]{:S(2)}, u32[]{:S(2)}) collective-permute-start(bf16[392,512]{1,0:T(8,128)(2,1)S(1)} %get-tuple-element.28), channel_id=1, source_target_pairs={{0,1},{1,2},{2,3},{3,0},{4,5},{5,6},{6,7},{7,4},{8,9},{9,10},{10,1... | collective-permute-start | bytes 1204232 | tf_op jit(solution)/shard_map/ppermute | solution.py:339
  8.0 1.5 %collective-permute-start.1 = (bf16[392,512]{1,0:T(8,128)(2,1)S(1)}, bf16[392,512]{1,0:T(8,128)(2,1)S(1)}, u32[]{:S(2)}, u32[]{:S(2)}) collective-permute-start(bf16[392,512]{1,0:T(8,128)(2,1)S(1)} %get-tuple-element.29), channel_id=1, source_target_pairs={{0,3},{1,0},{2,1},{3,2},{4,7},{5,4},{6,5},{7,6},{8,11},{9,8},{10,9... | collective-permute-start | bytes 1204232 | tf_op jit(solution)/shard_map/ppermute | solution.py:339
  9.5 5.0 %direct_windows.1 = (bf16[392,512]{1,0:T(8,128)(2,1)S(1)}, bf16[392,512]{1,0:T(8,128)(2,1)S(1)}, bf16[640,2048]{1,0:T(8,128)(2,1)S(1)}, bf16[640,2048]{1,0:T(8,128)(2,1)S(1)}) custom-call(bf16[672,2048]{1,0:T(8,128)(2,1)S(1)} %get-tuple-element.25.hg_ref, f32[672,128]{1,0:T(8,128)S(1)} %get-tuple-element.24.sq_ref, bf16[2376,2048]{1,0:T(8,128)(2,1)} %bitcast.4), custom_call_target="tpu_custom_call" | custom-call | flops 1761607680 | bytes 10000000 | tf_op jit(solution)/shard_map/direct_windows/pallas_call | solution.py:342
  14.5 0.1 collective-permute-start.2
  14.6 2.7 %collective-permute-start.3 = (bf16[392,512]{1,0:T(8,128)(2,1)S(1)}, bf16[392,512]{1,0:T(8,128)(2,1)S(1)}, u32[]{:S(2)}, u32[]{:S(2)}) collective-permute-start(bf16[392,512]{1,0:T(8,128)(2,1)S(1)} %get-tuple-element.32), channel_id=1, source_target_pairs={{0,3},{1,0},{2,1},{3,2},{4,7},{5,4},{6,5},{7,6},{8,11},{9,8},{10,9... | collective-permute-start | bytes 1204232 | tf_op jit(solution)/shard_map/ppermute | solution.py:339
  17.2 0.0 collective-permute-done.up_in_ref
  17.2 0.3 collective-permute-done.1.down_in_ref
  17.5 0.0 copy-start
  17.5 4.2 %passing_windows.1 = (bf16[280,512]{1,0:T(8,128)(2,1)S(1)}, bf16[280,512]{1,0:T(8,128)(2,1)S(1)}, bf16[112,512]{1,0:T(8,128)(2,1)S(1)}, bf16[112,512]{1,0:T(8,128)(2,1)S(1)}, bf16[640,2048]{1,0:T(8,128)(2,1)S(1)}) custom-call(bf16[672,2048]{1,0:T(8,128)(2,1)S(1)} %get-tuple-element.25.hg_ref, f32[672,128]{1,0:T(8,128)S(1)} %get-tuple-element.24.sq_ref, ...), custom_call_target="tpu_custom_call" | custom-call | flops 1761607680 | bytes 10000000 | tf_op jit(solution)/shard_map/passing_windows/pallas_call | solution.py:353
  21.7 1.6 %collective-permute-start.4 = (bf16[280,512]{1,0:T(8,128)(2,1)S(1)}, bf16[280,512]{1,0:T(8,128)(2,1)S(1)}, u32[]{:S(2)}, u32[]{:S(2)}) collective-permute-start(bf16[280,512]{1,0:T(8,128)(2,1)S(1)} %get-tuple-element.36), channel_id=1, source_target_pairs={{0,1},{1,2},{2,3},{3,0},{4,5},{5,6},{6,7},{7,4},{8,9},{9,10},{10,1... | collective-permute-start | bytes 860168 | tf_op jit(solution)/shard_map/ppermute | solution.py:339
  23.4 1.1 %collective-permute-start.5 = (bf16[280,512]{1,0:T(8,128)(2,1)S(1)}, bf16[280,512]{1,0:T(8,128)(2,1)S(1)}, u32[]{:S(2)}, u32[]{:S(2)}) collective-permute-start(bf16[280,512]{1,0:T(8,128)(2,1)S(1)} %get-tuple-element.37), channel_id=1, source_target_pairs={{0,3},{1,0},{2,1},{3,2},{4,7},{5,4},{6,5},{7,6},{8,11},{9,8},{10,9... | collective-permute-start | bytes 860168 | tf_op jit(solution)/shard_map/ppermute | solution.py:339
  24.5 0.0 copy-done
  24.5 0.4 collective-permute-start.6
  24.9 0.4 collective-permute-done.2.up_ref
  25.3 2.9 %collective-permute-start.7 = (bf16[112,512]{1,0:T(8,128)(2,1)S(1)}, bf16[112,512]{1,0:T(8,128)(2,1)S(1)}, u32[]{:S(2)}, u32[]{:S(2)}) collective-permute-start(bf16[112,512]{1,0:T(8,128)(2,1)S(1)} %get-tuple-element.40), channel_id=1, source_target_pairs={{0,3},{1,0},{2,1},{3,2},{4,7},{5,4},{6,5},{7,6},{8,11},{9,8},{10,9... | collective-permute-start | bytes 344072 | tf_op jit(solution)/shard_map/ppermute | solution.py:339
  28.1 2.3 %own_window.1.own_ref = f32[672,640]{1,0:T(8,128)S(1)} custom-call(bf16[672,2048]{1,0:T(8,128)(2,1)S(1)} %get-tuple-element.25.hg_ref, bf16[640,2048]{1,0:T(8,128)(2,1)S(1)} %get-tuple-element.30.w_own_ref), custom_call_target="tpu_custom_call" | custom-call | flops 1761607680 | bytes 6000000 | tf_op jit(solution)/shard_map/own_window/pallas_call | solution.py:365
  30.5 0.0 collective-permute-done.3.down_ref
  30.5 0.9 %own_and_direct.1 = (f32[672,640]{1,0:T(8,128)S(1)}, f32[672,128]{1,0:T(8,128)S(1)}, s32[672,128]{1,0:T(8,128)S(1)}) custom-call(s32[1,672]{1,0:T(1,128)S(1)} %reshape.13.ids_ref, f32[672,128]{1,0:T(8,128)S(1)} %get-tuple-element.24.sq_ref, f32[672,640]{1,0:T(8,128)S(1)} %own_window.1.own_ref, bf16[392,512]{1,0:T(8,128)(2,1)S(1)} %collective-permute-done.2.up_ref, ...), custom_call_target="tpu_custom_call" | custom-call | flops 1720320 | bytes 5000000 | tf_op jit(solution)/shard_map/own_and_direct/pallas_call | solution.py:374
  31.4 0.3 collective-permute-done.4.up_ref
  31.7 0.0 collective-permute-done.5.down_ref
  31.7 1.4 %early_totals.1 = (f32[480,640]{1,0:T(8,128)S(1)}, f32[16,128]{1,0:T(8,128)S(1)}) custom-call(f32[672,640]{1,0:T(8,128)S(1)} %get-tuple-element.33.sum_ref, f32[672,128]{1,0:T(8,128)S(1)} %get-tuple-element.34.part_ref, s32[672,128]{1,0:T(8,128)S(1)} %get-tuple-element.35.target_ref, bf16[280,512]{1,0:T(8,128)(2,1)S(1)} %collective-permute-done.4.up_ref, ...), custom_call_target="tpu_custom_call" | custom-call | tf_op jit(solution)/shard_map/early_totals/pallas_call | solution.py:384
  33.1 1.1 %collective-permute-done.6.up_ref = bf16[112,512]{1,0:T(8,128)(2,1)S(1)} collective-permute-done((bf16[112,512]{1,0:T(8,128)(2,1)S(1)}, bf16[112,512]{1,0:T(8,128)(2,1)S(1)}, u32[]{:S(2)}, u32[]{:S(2)}) %collective-permute-start.6) | collective-permute-done | bytes 114720 | tf_op jit(solution)/shard_map/ppermute | solution.py:339
  34.2 0.0 collective-permute-done.7.down_ref
  34.2 0.6 late_totals.1
  34.8 20.3 %all_to_all.10.parts_ref = f32[16,16,128]{2,1,0:T(8,128)S(1)} all-to-all(f32[16,16,128]{2,1,0:T(8,128)S(1)} %get-tuple-element.43), channel_id=1, replica_groups=mesh['section'=4,'tp'=16,'dp'=4] {'tp'}, dimensions={0} | all-to-all | bytes 262144 | tf_op jit(solution)/shard_map/all_to_all | solution.py:402
  55.1 0.1 join_totals.1
  55.2 12.9 %all_to_all.11.parts_ref = f32[16,8,128]{2,1,0:T(8,128)S(1)} all-to-all(f32[16,8,128]{2,1,0:T(8,128)S(1)} %join_totals.1), channel_id=1, replica_groups=mesh['section'=4,'tp'=16,'dp'=4] {'section','dp'}, dimensions={0} | all-to-all | bytes 131072 | tf_op jit(solution)/shard_map/all_to_all | solution.py:411
  68.1 1.6 %log_probabilities.1 = (bf16[672,594]{1,0:T(8,128)(2,1)}, f32[1,168]{1,0:T(1,128)}) custom-call(f32[480,640]{1,0:T(8,128)S(1)} %get-tuple-element.38.early_ref, f32[192,640]{1,0:T(8,128)S(1)} %get-tuple-element.42.late_ref, f32[16,8,128]{2,1,0:T(8,128)S(1)} %all_to_all.11.parts_ref), custom_call_target="tpu_custom_call" | custom-call | tf_op jit(solution)/shard_map/log_probabilities/pallas_call | solution.py:412
  (1 shorter events, 0.0 us)
Async XLA Ops:
  5.8 11.5 %collective-permute-start = (bf16[392,512]{1,0:T(8,128)(2,1)S(1)}, bf16[392,512]{1,0:T(8,128)(2,1)S(1)}, u32[]{:S(2)}, u32[]{:S(2)}) collective-permute-start(bf16[392,512]{1,0:T(8,128)(2,1)S(1)} %get-tuple-element.28), channel_id=1, source_target_pairs={{0,1},{1,2},{2,3},{3,0},{4,5},{5,6},{6,7},{7,4},{8,9},{9,10},{10,1... | collective-permute-start | bytes 1204232 | tf_op jit(solution)/shard_map/ppermute | solution.py:339
  8.0 9.6 %collective-permute-start.1 = (bf16[392,512]{1,0:T(8,128)(2,1)S(1)}, bf16[392,512]{1,0:T(8,128)(2,1)S(1)}, u32[]{:S(2)}, u32[]{:S(2)}) collective-permute-start(bf16[392,512]{1,0:T(8,128)(2,1)S(1)} %get-tuple-element.29), channel_id=1, source_target_pairs={{0,3},{1,0},{2,1},{3,2},{4,7},{5,4},{6,5},{7,6},{8,11},{9,8},{10,9... | collective-permute-start | bytes 1204232 | tf_op jit(solution)/shard_map/ppermute | solution.py:339
  14.5 10.8 %collective-permute-start.2 = (bf16[392,512]{1,0:T(8,128)(2,1)S(1)}, bf16[392,512]{1,0:T(8,128)(2,1)S(1)}, u32[]{:S(2)}, u32[]{:S(2)}) collective-permute-start(bf16[392,512]{1,0:T(8,128)(2,1)S(1)} %get-tuple-element.31), channel_id=1, source_target_pairs={{0,1},{1,2},{2,3},{3,0},{4,5},{5,6},{6,7},{7,4},{8,9},{9,10},{10,1... | collective-permute-start | bytes 1204232 | tf_op jit(solution)/shard_map/ppermute | solution.py:339
  14.6 15.9 %collective-permute-start.3 = (bf16[392,512]{1,0:T(8,128)(2,1)S(1)}, bf16[392,512]{1,0:T(8,128)(2,1)S(1)}, u32[]{:S(2)}, u32[]{:S(2)}) collective-permute-start(bf16[392,512]{1,0:T(8,128)(2,1)S(1)} %get-tuple-element.32), channel_id=1, source_target_pairs={{0,3},{1,0},{2,1},{3,2},{4,7},{5,4},{6,5},{7,6},{8,11},{9,8},{10,9... | collective-permute-start | bytes 1204232 | tf_op jit(solution)/shard_map/ppermute | solution.py:339
  17.5 7.0 %copy-start = (s32[672]{0:T(1024)S(1)}, s32[672]{0:T(1024)}, u32[]{:S(2)}) copy-start(s32[672]{0:T(1024)} %param.7) | copy-start | bytes 8068
  21.7 10.0 %collective-permute-start.4 = (bf16[280,512]{1,0:T(8,128)(2,1)S(1)}, bf16[280,512]{1,0:T(8,128)(2,1)S(1)}, u32[]{:S(2)}, u32[]{:S(2)}) collective-permute-start(bf16[280,512]{1,0:T(8,128)(2,1)S(1)} %get-tuple-element.36), channel_id=1, source_target_pairs={{0,1},{1,2},{2,3},{3,0},{4,5},{5,6},{6,7},{7,4},{8,9},{9,10},{10,1... | collective-permute-start | bytes 860168 | tf_op jit(solution)/shard_map/ppermute | solution.py:339
  23.4 8.3 %collective-permute-start.5 = (bf16[280,512]{1,0:T(8,128)(2,1)S(1)}, bf16[280,512]{1,0:T(8,128)(2,1)S(1)}, u32[]{:S(2)}, u32[]{:S(2)}) collective-permute-start(bf16[280,512]{1,0:T(8,128)(2,1)S(1)} %get-tuple-element.37), channel_id=1, source_target_pairs={{0,3},{1,0},{2,1},{3,2},{4,7},{5,4},{6,5},{7,6},{8,11},{9,8},{10,9... | collective-permute-start | bytes 860168 | tf_op jit(solution)/shard_map/ppermute | solution.py:339
  24.5 9.7 %collective-permute-start.6 = (bf16[112,512]{1,0:T(8,128)(2,1)S(1)}, bf16[112,512]{1,0:T(8,128)(2,1)S(1)}, u32[]{:S(2)}, u32[]{:S(2)}) collective-permute-start(bf16[112,512]{1,0:T(8,128)(2,1)S(1)} %get-tuple-element.39), channel_id=1, source_target_pairs={{0,1},{1,2},{2,3},{3,0},{4,5},{5,6},{6,7},{7,4},{8,9},{9,10},{10,1... | collective-permute-start | bytes 344072 | tf_op jit(solution)/shard_map/ppermute | solution.py:339
  25.3 8.9 %collective-permute-start.7 = (bf16[112,512]{1,0:T(8,128)(2,1)S(1)}, bf16[112,512]{1,0:T(8,128)(2,1)S(1)}, u32[]{:S(2)}, u32[]{:S(2)}) collective-permute-start(bf16[112,512]{1,0:T(8,128)(2,1)S(1)} %get-tuple-element.40), channel_id=1, source_target_pairs={{0,3},{1,0},{2,1},{3,2},{4,7},{5,4},{6,5},{7,6},{8,11},{9,8},{10,9... | collective-permute-start | bytes 344072 | tf_op jit(solution)/shard_map/ppermute | solution.py:339

commit v5 on v4

--- a/solution.py
+++ b/solution.py
@@ -78,7 +78,7 @@
 
 
 def message(rows):
-    return pltpu.VMEM((rows + rows // 6, LAST), BF16)
+    return pltpu.VMEM(((rows + rows // 6 + 15) // 16 * 16, LAST), BF16)
 
 
 def pack(out_ref, logits, squares):
@@ -100,7 +100,7 @@
     for i in (0, 1):
         for j, tile in enumerate((first, second)):
             begin = 256 * i + 128 * j
-            out_ref[n:, begin : begin + 128] = tile[i * sixth : i * sixth + sixth].astype(BF16)
+            out_ref[n : n + sixth, begin : begin + 128] = tile[i * sixth : i * sixth + sixth].astype(BF16)
 
 
 def unpack(in_ref, n):

time: 70.1 us -> 70.6 us (level)
  waiting for transfers between devices: 2.09 us -> 2.94 us
    ppermute x8, waiting for transfers between devices: 2.09 us -> 2.94 us  [shifted(): return lax.ppermute(array, 'dp', [(i, (i + k) % DP) for i in range(DP)])]
  transfers between devices with their start and end apart: 8 -> 8, of which waited for: 4 -> 6; matrix products, arithmetic and copies ran while one was open for 0% -> 0% of each run, Pallas kernels for 20% -> 20%
where the time goes in v5:
time: 70.6 us; the launch traced here: 70.4 us
  blocking collectives  33.1 us (47%)
  Pallas kernels  21.2 us (30%)
  starting transfers between devices  12.3 us (17%)
  waiting for transfers between devices  2.94 us (4%)
  between operations  0.87 us (1%)
    all_to_all x1, blocking collectives, body(): parts = lax.all_to_all(parts, 'tp', 0, 0, tiled=True)  20.2 us
    all_to_all x1, blocking collectives, body(): parts = lax.all_to_all(parts, ('section', 'dp'), 0, 0, tiled=True)  12.9 us
    ppermute x8, starting transfers between devices, shifted(): return lax.ppermute(array, 'dp', [(i, (i + k) % DP) for i in range(DP)])  12.3 us
    pallas_call x1, Pallas kernels, body(): pl.pallas_call(first_kernel, in_specs=[far(), far(), far()], out_specs=[w...  5.12 us
    pallas_call x1, Pallas kernels, body(): pl.pallas_call(direct_kernel, in_specs=[whole()] * 2 + [far()], out_specs...  4.99 us
    pallas_call x1, Pallas kernels, body(): pl.pallas_call(passing_kernel, in_specs=[whole()] * 6 + [far()], out_spec...  4.19 us
    ppermute x8, waiting for transfers between devices, shifted(): return lax.ppermute(array, 'dp', [(i, (i + k) % DP) for i in range(DP)])  2.94 us
    pallas_call x1, Pallas kernels, body(): pl.pallas_call(own_kernel, in_specs=[whole()] * 2, out_specs=whole(), out...  2.33 us
  transfers between devices with their start and end apart: 8, of which 6 were waited for; matrix products, arithmetic and copies ran while one was open for 0% of the time, Pallas kernels for 20%

profile of v5, /device:TPU:1, one launch (start us, length us, event | category | flops | bytes accessed | tf_op | source)
XLA Modules:
  0.0 70.4 jit_solution(7321564013945958947)
XLA Ops:
  0.6 5.1 %first_window.1 = (bf16[672,2048]{1,0:T(8,128)(2,1)S(1)}, f32[672,128]{1,0:T(8,128)S(1)}, bf16[400,512]{1,0:T(8,128)(2,1)S(1)}, bf16[400,512]{1,0:T(8,128)(2,1)S(1)}) custom-call(bf16[672,2048]{1,0:T(8,128)(2,1)} %x_ref.1, f32[1,2048]{1,0:T(1,128)} %bitcast.6, bf16[2376,2048]{1,0:T(8,128)(2,1)} %bitcast.3), custom_call_target="tpu_custom_call" | custom-call | flops 1761607680 | bytes 10000000 | tf_op jit(solution)/shard_map/first_window/pallas_call | solution.py:322
  5.8 2.2 %collective-permute-start = (bf16[400,512]{1,0:T(8,128)(2,1)S(1)}, bf16[400,512]{1,0:T(8,128)(2,1)S(1)}, u32[]{:S(2)}, u32[]{:S(2)}) collective-permute-start(bf16[400,512]{1,0:T(8,128)(2,1)S(1)} %get-tuple-element.28), channel_id=1, source_target_pairs={{0,1},{1,2},{2,3},{3,0},{4,5},{5,6},{6,7},{7,4},{8,9},{9,10},{10,1... | collective-permute-start | bytes 1228808 | tf_op jit(solution)/shard_map/ppermute | solution.py:339
  8.0 1.5 %collective-permute-start.1 = (bf16[400,512]{1,0:T(8,128)(2,1)S(1)}, bf16[400,512]{1,0:T(8,128)(2,1)S(1)}, u32[]{:S(2)}, u32[]{:S(2)}) collective-permute-start(bf16[400,512]{1,0:T(8,128)(2,1)S(1)} %get-tuple-element.29), channel_id=1, source_target_pairs={{0,3},{1,0},{2,1},{3,2},{4,7},{5,4},{6,5},{7,6},{8,11},{9,8},{10,9... | collective-permute-start | bytes 1228808 | tf_op jit(solution)/shard_map/ppermute | solution.py:339
  9.5 5.0 %direct_windows.1 = (bf16[400,512]{1,0:T(8,128)(2,1)S(1)}, bf16[400,512]{1,0:T(8,128)(2,1)S(1)}, bf16[640,2048]{1,0:T(8,128)(2,1)S(1)}, bf16[640,2048]{1,0:T(8,128)(2,1)S(1)}) custom-call(bf16[672,2048]{1,0:T(8,128)(2,1)S(1)} %get-tuple-element.25.hg_ref, f32[672,128]{1,0:T(8,128)S(1)} %get-tuple-element.24.sq_ref, bf16[2376,2048]{1,0:T(8,128)(2,1)} %bitcast.4), custom_call_target="tpu_custom_call" | custom-call | flops 1761607680 | bytes 10000000 | tf_op jit(solution)/shard_map/direct_windows/pallas_call | solution.py:342
  14.5 0.1 collective-permute-start.2
  14.6 2.7 %collective-permute-start.3 = (bf16[400,512]{1,0:T(8,128)(2,1)S(1)}, bf16[400,512]{1,0:T(8,128)(2,1)S(1)}, u32[]{:S(2)}, u32[]{:S(2)}) collective-permute-start(bf16[400,512]{1,0:T(8,128)(2,1)S(1)} %get-tuple-element.32), channel_id=1, source_target_pairs={{0,3},{1,0},{2,1},{3,2},{4,7},{5,4},{6,5},{7,6},{8,11},{9,8},{10,9... | collective-permute-start | bytes 1228808 | tf_op jit(solution)/shard_map/ppermute | solution.py:339
  17.2 0.0 collective-permute-done.up_in_ref
  17.2 0.5 collective-permute-done.1.down_in_ref
  17.7 0.0 copy-start
  17.7 4.2 %passing_windows.1 = (bf16[288,512]{1,0:T(8,128)(2,1)S(1)}, bf16[288,512]{1,0:T(8,128)(2,1)S(1)}, bf16[112,512]{1,0:T(8,128)(2,1)S(1)}, bf16[112,512]{1,0:T(8,128)(2,1)S(1)}, bf16[640,2048]{1,0:T(8,128)(2,1)S(1)}) custom-call(bf16[672,2048]{1,0:T(8,128)(2,1)S(1)} %get-tuple-element.25.hg_ref, f32[672,128]{1,0:T(8,128)S(1)} %get-tuple-element.24.sq_ref, ...), custom_call_target="tpu_custom_call" | custom-call | flops 1761607680 | bytes 10000000 | tf_op jit(solution)/shard_map/passing_windows/pallas_call | solution.py:353
  21.9 1.6 %collective-permute-start.4 = (bf16[288,512]{1,0:T(8,128)(2,1)S(1)}, bf16[288,512]{1,0:T(8,128)(2,1)S(1)}, u32[]{:S(2)}, u32[]{:S(2)}) collective-permute-start(bf16[288,512]{1,0:T(8,128)(2,1)S(1)} %get-tuple-element.36), channel_id=1, source_target_pairs={{0,1},{1,2},{2,3},{3,0},{4,5},{5,6},{6,7},{7,4},{8,9},{9,10},{10,1... | collective-permute-start | bytes 884744 | tf_op jit(solution)/shard_map/ppermute | solution.py:339
  23.5 1.1 %collective-permute-start.5 = (bf16[288,512]{1,0:T(8,128)(2,1)S(1)}, bf16[288,512]{1,0:T(8,128)(2,1)S(1)}, u32[]{:S(2)}, u32[]{:S(2)}) collective-permute-start(bf16[288,512]{1,0:T(8,128)(2,1)S(1)} %get-tuple-element.37), channel_id=1, source_target_pairs={{0,3},{1,0},{2,1},{3,2},{4,7},{5,4},{6,5},{7,6},{8,11},{9,8},{10,9... | collective-permute-start | bytes 884744 | tf_op jit(solution)/shard_map/ppermute | solution.py:339
  24.7 0.0 copy-done
  24.7 0.3 collective-permute-start.6
  25.0 0.8 %collective-permute-done.2.up_ref = bf16[400,512]{1,0:T(8,128)(2,1)S(1)} collective-permute-done((bf16[400,512]{1,0:T(8,128)(2,1)S(1)}, bf16[400,512]{1,0:T(8,128)(2,1)S(1)}, u32[]{:S(2)}, u32[]{:S(2)}) %collective-permute-start.2) | collective-permute-done | bytes 409632 | tf_op jit(solution)/shard_map/ppermute | solution.py:339
  25.8 2.7 %collective-permute-start.7 = (bf16[112,512]{1,0:T(8,128)(2,1)S(1)}, bf16[112,512]{1,0:T(8,128)(2,1)S(1)}, u32[]{:S(2)}, u32[]{:S(2)}) collective-permute-start(bf16[112,512]{1,0:T(8,128)(2,1)S(1)} %get-tuple-element.40), channel_id=1, source_target_pairs={{0,3},{1,0},{2,1},{3,2},{4,7},{5,4},{6,5},{7,6},{8,11},{9,8},{10,9... | collective-permute-start | bytes 344072 | tf_op jit(solution)/shard_map/ppermute | solution.py:339
  28.5 2.3 %own_window.1.own_ref = f32[672,640]{1,0:T(8,128)S(1)} custom-call(bf16[672,2048]{1,0:T(8,128)(2,1)S(1)} %get-tuple-element.25.hg_ref, bf16[640,2048]{1,0:T(8,128)(2,1)S(1)} %get-tuple-element.30.w_own_ref), custom_call_target="tpu_custom_call" | custom-call | flops 1761607680 | bytes 6000000 | tf_op jit(solution)/shard_map/own_window/pallas_call | solution.py:365
  30.8 0.0 collective-permute-done.3.down_ref
  30.8 0.9 %own_and_direct.1 = (f32[672,640]{1,0:T(8,128)S(1)}, f32[672,128]{1,0:T(8,128)S(1)}, s32[672,128]{1,0:T(8,128)S(1)}) custom-call(s32[1,672]{1,0:T(1,128)S(1)} %reshape.13.ids_ref, f32[672,128]{1,0:T(8,128)S(1)} %get-tuple-element.24.sq_ref, f32[672,640]{1,0:T(8,128)S(1)} %own_window.1.own_ref, bf16[400,512]{1,0:T(8,128)(2,1)S(1)} %collective-permute-done.2.up_ref, ...), custom_call_target="tpu_custom_call" | custom-call | flops 1720320 | bytes 5000000 | tf_op jit(solution)/shard_map/own_and_direct/pallas_call | solution.py:374
  31.7 0.5 collective-permute-done.4.up_ref
  32.3 0.1 collective-permute-done.5.down_ref
  32.4 1.4 %early_totals.1 = (f32[480,640]{1,0:T(8,128)S(1)}, f32[16,128]{1,0:T(8,128)S(1)}) custom-call(f32[672,640]{1,0:T(8,128)S(1)} %get-tuple-element.33.sum_ref, f32[672,128]{1,0:T(8,128)S(1)} %get-tuple-element.34.part_ref, s32[672,128]{1,0:T(8,128)S(1)} %get-tuple-element.35.target_ref, bf16[288,512]{1,0:T(8,128)(2,1)S(1)} %collective-permute-done.4.up_ref, ...), custom_call_target="tpu_custom_call" | custom-call | tf_op jit(solution)/shard_map/early_totals/pallas_call | solution.py:384
  33.8 1.0 %collective-permute-done.6.up_ref = bf16[112,512]{1,0:T(8,128)(2,1)S(1)} collective-permute-done((bf16[112,512]{1,0:T(8,128)(2,1)S(1)}, bf16[112,512]{1,0:T(8,128)(2,1)S(1)}, u32[]{:S(2)}, u32[]{:S(2)}) %collective-permute-start.6) | collective-permute-done | bytes 114720 | tf_op jit(solution)/shard_map/ppermute | solution.py:339
  34.7 0.1 collective-permute-done.7.down_ref
  34.8 0.6 late_totals.1
  35.4 20.2 %all_to_all.10.parts_ref = f32[16,16,128]{2,1,0:T(8,128)S(1)} all-to-all(f32[16,16,128]{2,1,0:T(8,128)S(1)} %get-tuple-element.43), channel_id=1, replica_groups=mesh['section'=4,'tp'=16,'dp'=4] {'tp'}, dimensions={0} | all-to-all | bytes 262144 | tf_op jit(solution)/shard_map/all_to_all | solution.py:402
  55.6 0.1 join_totals.1
  55.7 12.9 %all_to_all.11.parts_ref = f32[16,8,128]{2,1,0:T(8,128)S(1)} all-to-all(f32[16,8,128]{2,1,0:T(8,128)S(1)} %join_totals.1), channel_id=1, replica_groups=mesh['section'=4,'tp'=16,'dp'=4] {'section','dp'}, dimensions={0} | all-to-all | bytes 131072 | tf_op jit(solution)/shard_map/all_to_all | solution.py:411
  68.6 1.6 %log_probabilities.1 = (bf16[672,594]{1,0:T(8,128)(2,1)}, f32[1,168]{1,0:T(1,128)}) custom-call(f32[480,640]{1,0:T(8,128)S(1)} %get-tuple-element.38.early_ref, f32[192,640]{1,0:T(8,128)S(1)} %get-tuple-element.42.late_ref, f32[16,8,128]{2,1,0:T(8,128)S(1)} %all_to_all.11.parts_ref), custom_call_target="tpu_custom_call" | custom-call | tf_op jit(solution)/shard_map/log_probabilities/pallas_call | solution.py:412
  (1 shorter events, 0.0 us)
Async XLA Ops:
  5.8 11.5 %collective-permute-start = (bf16[400,512]{1,0:T(8,128)(2,1)S(1)}, bf16[400,512]{1,0:T(8,128)(2,1)S(1)}, u32[]{:S(2)}, u32[]{:S(2)}) collective-permute-start(bf16[400,512]{1,0:T(8,128)(2,1)S(1)} %get-tuple-element.28), channel_id=1, source_target_pairs={{0,1},{1,2},{2,3},{3,0},{4,5},{5,6},{6,7},{7,4},{8,9},{9,10},{10,1... | collective-permute-start | bytes 1228808 | tf_op jit(solution)/shard_map/ppermute | solution.py:339
  8.0 9.7 %collective-permute-start.1 = (bf16[400,512]{1,0:T(8,128)(2,1)S(1)}, bf16[400,512]{1,0:T(8,128)(2,1)S(1)}, u32[]{:S(2)}, u32[]{:S(2)}) collective-permute-start(bf16[400,512]{1,0:T(8,128)(2,1)S(1)} %get-tuple-element.29), channel_id=1, source_target_pairs={{0,3},{1,0},{2,1},{3,2},{4,7},{5,4},{6,5},{7,6},{8,11},{9,8},{10,9... | collective-permute-start | bytes 1228808 | tf_op jit(solution)/shard_map/ppermute | solution.py:339
  14.5 11.3 %collective-permute-start.2 = (bf16[400,512]{1,0:T(8,128)(2,1)S(1)}, bf16[400,512]{1,0:T(8,128)(2,1)S(1)}, u32[]{:S(2)}, u32[]{:S(2)}) collective-permute-start(bf16[400,512]{1,0:T(8,128)(2,1)S(1)} %get-tuple-element.31), channel_id=1, source_target_pairs={{0,1},{1,2},{2,3},{3,0},{4,5},{5,6},{6,7},{7,4},{8,9},{9,10},{10,1... | collective-permute-start | bytes 1228808 | tf_op jit(solution)/shard_map/ppermute | solution.py:339
  14.6 16.3 %collective-permute-start.3 = (bf16[400,512]{1,0:T(8,128)(2,1)S(1)}, bf16[400,512]{1,0:T(8,128)(2,1)S(1)}, u32[]{:S(2)}, u32[]{:S(2)}) collective-permute-start(bf16[400,512]{1,0:T(8,128)(2,1)S(1)} %get-tuple-element.32), channel_id=1, source_target_pairs={{0,3},{1,0},{2,1},{3,2},{4,7},{5,4},{6,5},{7,6},{8,11},{9,8},{10,9... | collective-permute-start | bytes 1228808 | tf_op jit(solution)/shard_map/ppermute | solution.py:339
  17.7 7.0 %copy-start = (s32[672]{0:T(1024)S(1)}, s32[672]{0:T(1024)}, u32[]{:S(2)}) copy-start(s32[672]{0:T(1024)} %param.7) | copy-start | bytes 8068
  21.9 10.4 %collective-permute-start.4 = (bf16[288,512]{1,0:T(8,128)(2,1)S(1)}, bf16[288,512]{1,0:T(8,128)(2,1)S(1)}, u32[]{:S(2)}, u32[]{:S(2)}) collective-permute-start(bf16[288,512]{1,0:T(8,128)(2,1)S(1)} %get-tuple-element.36), channel_id=1, source_target_pairs={{0,1},{1,2},{2,3},{3,0},{4,5},{5,6},{6,7},{7,4},{8,9},{9,10},{10,1... | collective-permute-start | bytes 884744 | tf_op jit(solution)/shard_map/ppermute | solution.py:339
  23.5 8.8 %collective-permute-start.5 = (bf16[288,512]{1,0:T(8,128)(2,1)S(1)}, bf16[288,512]{1,0:T(8,128)(2,1)S(1)}, u32[]{:S(2)}, u32[]{:S(2)}) collective-permute-start(bf16[288,512]{1,0:T(8,128)(2,1)S(1)} %get-tuple-element.37), channel_id=1, source_target_pairs={{0,3},{1,0},{2,1},{3,2},{4,7},{5,4},{6,5},{7,6},{8,11},{9,8},{10,9... | collective-permute-start | bytes 884744 | tf_op jit(solution)/shard_map/ppermute | solution.py:339
  24.7 10.1 %collective-permute-start.6 = (bf16[112,512]{1,0:T(8,128)(2,1)S(1)}, bf16[112,512]{1,0:T(8,128)(2,1)S(1)}, u32[]{:S(2)}, u32[]{:S(2)}) collective-permute-start(bf16[112,512]{1,0:T(8,128)(2,1)S(1)} %get-tuple-element.39), channel_id=1, source_target_pairs={{0,1},{1,2},{2,3},{3,0},{4,5},{5,6},{6,7},{7,4},{8,9},{9,10},{10,1... | collective-permute-start | bytes 344072 | tf_op jit(solution)/shard_map/ppermute | solution.py:339
  25.8 9.0 %collective-permute-start.7 = (bf16[112,512]{1,0:T(8,128)(2,1)S(1)}, bf16[112,512]{1,0:T(8,128)(2,1)S(1)}, u32[]{:S(2)}, u32[]{:S(2)}) collective-permute-start(bf16[112,512]{1,0:T(8,128)(2,1)S(1)} %get-tuple-element.40), channel_id=1, source_target_pairs={{0,3},{1,0},{2,1},{3,2},{4,7},{5,4},{6,5},{7,6},{8,11},{9,8},{10,9... | collective-permute-start | bytes 344072 | tf_op jit(solution)/shard_map/ppermute | solution.py:339

commit v6 on v4

--- a/solution.py
+++ b/solution.py
@@ -209,9 +209,10 @@
     over, squares = unpack(came_ref, n)
     over_ref[...] = over
     scale_ref[...] = lax.rsqrt((part_ref[at : at + n, :] + squares) / D + EPSILON)
-    for begin in range(0, n, PIECE):
-        rows, part, out = (slice(start + begin, start + begin + PIECE) for start in (at, 0, to))
-        lane = lane_of((PIECE, 128))
+    piece = 80 if n == EARLY else 96
+    for begin in range(0, n, piece):
+        rows, part, out = (slice(start + begin, start + begin + piece) for start in (at, 0, to))
+        lane = lane_of((piece, 128))
         scale, target = scale_ref[part, :], target_ref[rows, :]
         tiles = []
         for k in range(0, WIDE, 128):
@@ -223,7 +224,7 @@
         for tile in tiles[1:]:
             top = jnp.maximum(top, tile)
         top = jnp.max(top, axis=1, keepdims=True)
-        total = picked = jnp.zeros((PIECE, 128), F32)
+        total = picked = jnp.zeros((piece, 128), F32)
         for k, tile in enumerate(tiles):
             total = total + jnp.exp(tile - top)
             picked = picked + jnp.where(lane == target - 128 * k, tile, 0.0)

time: 70.1 us -> 69.9 us (level)
  no operation moved by 1% of the time
where the time goes in v6:
time: 69.9 us; the launch traced here: 69.7 us
  blocking collectives  33.1 us (47%)
  Pallas kernels  21.1 us (30%)
  starting transfers between devices  12.5 us (18%)
  waiting for transfers between devices  2.26 us (3%)
  between operations  0.87 us (1%)
    all_to_all x1, blocking collectives, body(): parts = lax.all_to_all(parts, 'tp', 0, 0, tiled=True)  20.1 us
    all_to_all x1, blocking collectives, body(): parts = lax.all_to_all(parts, ('section', 'dp'), 0, 0, tiled=True)  12.9 us
    ppermute x8, starting transfers between devices, shifted(): return lax.ppermute(array, 'dp', [(i, (i + k) % DP) for i in range(DP)])  12.5 us
    pallas_call x1, Pallas kernels, body(): pl.pallas_call(first_kernel, in_specs=[far(), far(), far()], out_specs=[w...  5.12 us
    pallas_call x1, Pallas kernels, body(): pl.pallas_call(direct_kernel, in_specs=[whole()] * 2 + [far()], out_specs...  4.99 us
    pallas_call x1, Pallas kernels, body(): pl.pallas_call(passing_kernel, in_specs=[whole()] * 6 + [far()], out_spec...  4.2 us
    pallas_call x1, Pallas kernels, body(): pl.pallas_call(own_kernel, in_specs=[whole()] * 2, out_specs=whole(), out...  2.33 us
    ppermute x8, waiting for transfers between devices, shifted(): return lax.ppermute(array, 'dp', [(i, (i + k) % DP) for i in range(DP)])  2.26 us
  transfers between devices with their start and end apart: 8, of which 4 were waited for; matrix products, arithmetic and copies ran while one was open for 0% of the time, Pallas kernels for 20%

profile of v6, /device:TPU:1, one launch (start us, length us, event | category | flops | bytes accessed | tf_op | source)
XLA Modules:
  0.0 69.7 jit_solution(3037821236556600025)
XLA Ops:
  0.6 5.1 %first_window.1 = (bf16[672,2048]{1,0:T(8,128)(2,1)S(1)}, f32[672,128]{1,0:T(8,128)S(1)}, bf16[392,512]{1,0:T(8,128)(2,1)S(1)}, bf16[392,512]{1,0:T(8,128)(2,1)S(1)}) custom-call(bf16[672,2048]{1,0:T(8,128)(2,1)} %x_ref.1, f32[1,2048]{1,0:T(1,128)} %bitcast.6, bf16[2376,2048]{1,0:T(8,128)(2,1)} %bitcast.3), custom_call_target="tpu_custom_call" | custom-call | flops 1761607680 | bytes 10000000 | tf_op jit(solution)/shard_map/first_window/pallas_call | solution.py:323
  5.8 2.2 %collective-permute-start = (bf16[392,512]{1,0:T(8,128)(2,1)S(1)}, bf16[392,512]{1,0:T(8,128)(2,1)S(1)}, u32[]{:S(2)}, u32[]{:S(2)}) collective-permute-start(bf16[392,512]{1,0:T(8,128)(2,1)S(1)} %get-tuple-element.28), channel_id=1, source_target_pairs={{0,1},{1,2},{2,3},{3,0},{4,5},{5,6},{6,7},{7,4},{8,9},{9,10},{10,1... | collective-permute-start | bytes 1204232 | tf_op jit(solution)/shard_map/ppermute | solution.py:340
  8.0 1.5 %collective-permute-start.1 = (bf16[392,512]{1,0:T(8,128)(2,1)S(1)}, bf16[392,512]{1,0:T(8,128)(2,1)S(1)}, u32[]{:S(2)}, u32[]{:S(2)}) collective-permute-start(bf16[392,512]{1,0:T(8,128)(2,1)S(1)} %get-tuple-element.29), channel_id=1, source_target_pairs={{0,3},{1,0},{2,1},{3,2},{4,7},{5,4},{6,5},{7,6},{8,11},{9,8},{10,9... | collective-permute-start | bytes 1204232 | tf_op jit(solution)/shard_map/ppermute | solution.py:340
  9.5 5.0 %direct_windows.1 = (bf16[392,512]{1,0:T(8,128)(2,1)S(1)}, bf16[392,512]{1,0:T(8,128)(2,1)S(1)}, bf16[640,2048]{1,0:T(8,128)(2,1)S(1)}, bf16[640,2048]{1,0:T(8,128)(2,1)S(1)}) custom-call(bf16[672,2048]{1,0:T(8,128)(2,1)S(1)} %get-tuple-element.25.hg_ref, f32[672,128]{1,0:T(8,128)S(1)} %get-tuple-element.24.sq_ref, bf16[2376,2048]{1,0:T(8,128)(2,1)} %bitcast.4), custom_call_target="tpu_custom_call" | custom-call | flops 1761607680 | bytes 10000000 | tf_op jit(solution)/shard_map/direct_windows/pallas_call | solution.py:343
  14.5 0.1 collective-permute-start.2
  14.6 2.7 %collective-permute-start.3 = (bf16[392,512]{1,0:T(8,128)(2,1)S(1)}, bf16[392,512]{1,0:T(8,128)(2,1)S(1)}, u32[]{:S(2)}, u32[]{:S(2)}) collective-permute-start(bf16[392,512]{1,0:T(8,128)(2,1)S(1)} %get-tuple-element.32), channel_id=1, source_target_pairs={{0,3},{1,0},{2,1},{3,2},{4,7},{5,4},{6,5},{7,6},{8,11},{9,8},{10,9... | collective-permute-start | bytes 1204232 | tf_op jit(solution)/shard_map/ppermute | solution.py:340
  17.2 0.0 collective-permute-done.up_in_ref
  17.2 0.3 collective-permute-done.1.down_in_ref
  17.5 0.0 copy-start
  17.5 4.2 %passing_windows.1 = (bf16[280,512]{1,0:T(8,128)(2,1)S(1)}, bf16[280,512]{1,0:T(8,128)(2,1)S(1)}, bf16[112,512]{1,0:T(8,128)(2,1)S(1)}, bf16[112,512]{1,0:T(8,128)(2,1)S(1)}, bf16[640,2048]{1,0:T(8,128)(2,1)S(1)}) custom-call(bf16[672,2048]{1,0:T(8,128)(2,1)S(1)} %get-tuple-element.25.hg_ref, f32[672,128]{1,0:T(8,128)S(1)} %get-tuple-element.24.sq_ref, ...), custom_call_target="tpu_custom_call" | custom-call | flops 1761607680 | bytes 10000000 | tf_op jit(solution)/shard_map/passing_windows/pallas_call | solution.py:354
  21.7 1.6 %collective-permute-start.4 = (bf16[280,512]{1,0:T(8,128)(2,1)S(1)}, bf16[280,512]{1,0:T(8,128)(2,1)S(1)}, u32[]{:S(2)}, u32[]{:S(2)}) collective-permute-start(bf16[280,512]{1,0:T(8,128)(2,1)S(1)} %get-tuple-element.36), channel_id=1, source_target_pairs={{0,1},{1,2},{2,3},{3,0},{4,5},{5,6},{6,7},{7,4},{8,9},{9,10},{10,1... | collective-permute-start | bytes 860168 | tf_op jit(solution)/shard_map/ppermute | solution.py:340
  23.4 1.1 %collective-permute-start.5 = (bf16[280,512]{1,0:T(8,128)(2,1)S(1)}, bf16[280,512]{1,0:T(8,128)(2,1)S(1)}, u32[]{:S(2)}, u32[]{:S(2)}) collective-permute-start(bf16[280,512]{1,0:T(8,128)(2,1)S(1)} %get-tuple-element.37), channel_id=1, source_target_pairs={{0,3},{1,0},{2,1},{3,2},{4,7},{5,4},{6,5},{7,6},{8,11},{9,8},{10,9... | collective-permute-start | bytes 860168 | tf_op jit(solution)/shard_map/ppermute | solution.py:340
  24.5 0.0 copy-done
  24.5 0.4 collective-permute-start.6
  24.9 0.4 collective-permute-done.2.up_ref
  25.3 2.9 %collective-permute-start.7 = (bf16[112,512]{1,0:T(8,128)(2,1)S(1)}, bf16[112,512]{1,0:T(8,128)(2,1)S(1)}, u32[]{:S(2)}, u32[]{:S(2)}) collective-permute-start(bf16[112,512]{1,0:T(8,128)(2,1)S(1)} %get-tuple-element.40), channel_id=1, source_target_pairs={{0,3},{1,0},{2,1},{3,2},{4,7},{5,4},{6,5},{7,6},{8,11},{9,8},{10,9... | collective-permute-start | bytes 344072 | tf_op jit(solution)/shard_map/ppermute | solution.py:340
  28.1 2.3 %own_window.1.own_ref = f32[672,640]{1,0:T(8,128)S(1)} custom-call(bf16[672,2048]{1,0:T(8,128)(2,1)S(1)} %get-tuple-element.25.hg_ref, bf16[640,2048]{1,0:T(8,128)(2,1)S(1)} %get-tuple-element.30.w_own_ref), custom_call_target="tpu_custom_call" | custom-call | flops 1761607680 | bytes 6000000 | tf_op jit(solution)/shard_map/own_window/pallas_call | solution.py:366
  30.5 0.0 collective-permute-done.3.down_ref
  30.5 0.9 %own_and_direct.1 = (f32[672,640]{1,0:T(8,128)S(1)}, f32[672,128]{1,0:T(8,128)S(1)}, s32[672,128]{1,0:T(8,128)S(1)}) custom-call(s32[1,672]{1,0:T(1,128)S(1)} %reshape.13.ids_ref, f32[672,128]{1,0:T(8,128)S(1)} %get-tuple-element.24.sq_ref, f32[672,640]{1,0:T(8,128)S(1)} %own_window.1.own_ref, bf16[392,512]{1,0:T(8,128)(2,1)S(1)} %collective-permute-done.2.up_ref, ...), custom_call_target="tpu_custom_call" | custom-call | flops 1720320 | bytes 5000000 | tf_op jit(solution)/shard_map/own_and_direct/pallas_call | solution.py:375
  31.4 0.3 collective-permute-done.4.up_ref
  31.7 0.0 collective-permute-done.5.down_ref
  31.7 1.2 %early_totals.1 = (f32[480,640]{1,0:T(8,128)S(1)}, f32[16,128]{1,0:T(8,128)S(1)}) custom-call(f32[672,640]{1,0:T(8,128)S(1)} %get-tuple-element.33.sum_ref, f32[672,128]{1,0:T(8,128)S(1)} %get-tuple-element.34.part_ref, s32[672,128]{1,0:T(8,128)S(1)} %get-tuple-element.35.target_ref, bf16[280,512]{1,0:T(8,128)(2,1)S(1)} %collective-permute-done.4.up_ref, ...), custom_call_target="tpu_custom_call" | custom-call | tf_op jit(solution)/shard_map/early_totals/pallas_call | solution.py:385
  32.9 1.2 %collective-permute-done.6.up_ref = bf16[112,512]{1,0:T(8,128)(2,1)S(1)} collective-permute-done((bf16[112,512]{1,0:T(8,128)(2,1)S(1)}, bf16[112,512]{1,0:T(8,128)(2,1)S(1)}, u32[]{:S(2)}, u32[]{:S(2)}) %collective-permute-start.6) | collective-permute-done | bytes 114720 | tf_op jit(solution)/shard_map/ppermute | solution.py:340
  34.2 0.0 collective-permute-done.7.down_ref
  34.2 0.6 late_totals.1
  34.8 20.1 %all_to_all.10.parts_ref = f32[16,16,128]{2,1,0:T(8,128)S(1)} all-to-all(f32[16,16,128]{2,1,0:T(8,128)S(1)} %get-tuple-element.43), channel_id=1, replica_groups=mesh['section'=4,'tp'=16,'dp'=4] {'tp'}, dimensions={0} | all-to-all | bytes 262144 | tf_op jit(solution)/shard_map/all_to_all | solution.py:403
  54.9 0.1 join_totals.1
  55.0 12.9 %all_to_all.11.parts_ref = f32[16,8,128]{2,1,0:T(8,128)S(1)} all-to-all(f32[16,8,128]{2,1,0:T(8,128)S(1)} %join_totals.1), channel_id=1, replica_groups=mesh['section'=4,'tp'=16,'dp'=4] {'section','dp'}, dimensions={0} | all-to-all | bytes 131072 | tf_op jit(solution)/shard_map/all_to_all | solution.py:412
  67.9 1.6 %log_probabilities.1 = (bf16[672,594]{1,0:T(8,128)(2,1)}, f32[1,168]{1,0:T(1,128)}) custom-call(f32[480,640]{1,0:T(8,128)S(1)} %get-tuple-element.38.early_ref, f32[192,640]{1,0:T(8,128)S(1)} %get-tuple-element.42.late_ref, f32[16,8,128]{2,1,0:T(8,128)S(1)} %all_to_all.11.parts_ref), custom_call_target="tpu_custom_call" | custom-call | tf_op jit(solution)/shard_map/log_probabilities/pallas_call | solution.py:413
  (1 shorter events, 0.0 us)
Async XLA Ops:
  5.8 11.5 %collective-permute-start = (bf16[392,512]{1,0:T(8,128)(2,1)S(1)}, bf16[392,512]{1,0:T(8,128)(2,1)S(1)}, u32[]{:S(2)}, u32[]{:S(2)}) collective-permute-start(bf16[392,512]{1,0:T(8,128)(2,1)S(1)} %get-tuple-element.28), channel_id=1, source_target_pairs={{0,1},{1,2},{2,3},{3,0},{4,5},{5,6},{6,7},{7,4},{8,9},{9,10},{10,1... | collective-permute-start | bytes 1204232 | tf_op jit(solution)/shard_map/ppermute | solution.py:340
  8.0 9.6 %collective-permute-start.1 = (bf16[392,512]{1,0:T(8,128)(2,1)S(1)}, bf16[392,512]{1,0:T(8,128)(2,1)S(1)}, u32[]{:S(2)}, u32[]{:S(2)}) collective-permute-start(bf16[392,512]{1,0:T(8,128)(2,1)S(1)} %get-tuple-element.29), channel_id=1, source_target_pairs={{0,3},{1,0},{2,1},{3,2},{4,7},{5,4},{6,5},{7,6},{8,11},{9,8},{10,9... | collective-permute-start | bytes 1204232 | tf_op jit(solution)/shard_map/ppermute | solution.py:340
  14.5 10.8 %collective-permute-start.2 = (bf16[392,512]{1,0:T(8,128)(2,1)S(1)}, bf16[392,512]{1,0:T(8,128)(2,1)S(1)}, u32[]{:S(2)}, u32[]{:S(2)}) collective-permute-start(bf16[392,512]{1,0:T(8,128)(2,1)S(1)} %get-tuple-element.31), channel_id=1, source_target_pairs={{0,1},{1,2},{2,3},{3,0},{4,5},{5,6},{6,7},{7,4},{8,9},{9,10},{10,1... | collective-permute-start | bytes 1204232 | tf_op jit(solution)/shard_map/ppermute | solution.py:340
  14.6 15.9 %collective-permute-start.3 = (bf16[392,512]{1,0:T(8,128)(2,1)S(1)}, bf16[392,512]{1,0:T(8,128)(2,1)S(1)}, u32[]{:S(2)}, u32[]{:S(2)}) collective-permute-start(bf16[392,512]{1,0:T(8,128)(2,1)S(1)} %get-tuple-element.32), channel_id=1, source_target_pairs={{0,3},{1,0},{2,1},{3,2},{4,7},{5,4},{6,5},{7,6},{8,11},{9,8},{10,9... | collective-permute-start | bytes 1204232 | tf_op jit(solution)/shard_map/ppermute | solution.py:340
  17.5 7.0 %copy-start = (s32[672]{0:T(1024)S(1)}, s32[672]{0:T(1024)}, u32[]{:S(2)}) copy-start(s32[672]{0:T(1024)} %param.7) | copy-start | bytes 8068
  21.7 10.0 %collective-permute-start.4 = (bf16[280,512]{1,0:T(8,128)(2,1)S(1)}, bf16[280,512]{1,0:T(8,128)(2,1)S(1)}, u32[]{:S(2)}, u32[]{:S(2)}) collective-permute-start(bf16[280,512]{1,0:T(8,128)(2,1)S(1)} %get-tuple-element.36), channel_id=1, source_target_pairs={{0,1},{1,2},{2,3},{3,0},{4,5},{5,6},{6,7},{7,4},{8,9},{9,10},{10,1... | collective-permute-start | bytes 860168 | tf_op jit(solution)/shard_map/ppermute | solution.py:340
  23.4 8.3 %collective-permute-start.5 = (bf16[280,512]{1,0:T(8,128)(2,1)S(1)}, bf16[280,512]{1,0:T(8,128)(2,1)S(1)}, u32[]{:S(2)}, u32[]{:S(2)}) collective-permute-start(bf16[280,512]{1,0:T(8,128)(2,1)S(1)} %get-tuple-element.37), channel_id=1, source_target_pairs={{0,3},{1,0},{2,1},{3,2},{4,7},{5,4},{6,5},{7,6},{8,11},{9,8},{10,9... | collective-permute-start | bytes 860168 | tf_op jit(solution)/shard_map/ppermute | solution.py:340
  24.5 9.7 %collective-permute-start.6 = (bf16[112,512]{1,0:T(8,128)(2,1)S(1)}, bf16[112,512]{1,0:T(8,128)(2,1)S(1)}, u32[]{:S(2)}, u32[]{:S(2)}) collective-permute-start(bf16[112,512]{1,0:T(8,128)(2,1)S(1)} %get-tuple-element.39), channel_id=1, source_target_pairs={{0,1},{1,2},{2,3},{3,0},{4,5},{5,6},{6,7},{7,4},{8,9},{9,10},{10,1... | collective-permute-start | bytes 344072 | tf_op jit(solution)/shard_map/ppermute | solution.py:340
  25.3 8.9 %collective-permute-start.7 = (bf16[112,512]{1,0:T(8,128)(2,1)S(1)}, bf16[112,512]{1,0:T(8,128)(2,1)S(1)}, u32[]{:S(2)}, u32[]{:S(2)}) collective-permute-start(bf16[112,512]{1,0:T(8,128)(2,1)S(1)} %get-tuple-element.40), channel_id=1, source_target_pairs={{0,3},{1,0},{2,1},{3,2},{4,7},{5,4},{6,5},{7,6},{8,11},{9,8},{10,9... | collective-permute-start | bytes 344072 | tf_op jit(solution)/shard_map/ppermute | solution.py:340
